TPU v7x, 32 devices: a whole 2x2x4 slice. The times are simulated.
32 devices in a mesh: groups: 2 (over x), fsdp: 16 (over z, y, core).
Axes of the slice: x: 2, y: 2, z: 4, core: 2. Of those that a mesh axis runs over, the one named last changes fastest.
Arguments:
- expert_grad: float32 [8, 3, 768, 2048], P('groups', None, 'fsdp'), parts along dimension 0, may hold values from -12 to 12
- expert_momentum: float32 [8, 3, 768, 2048], P('groups', None, 'fsdp'), parts along dimension 0, may hold values from -6 to 6
- expert_master: float32 [8, 3, 768, 2048], P('groups', None, 'fsdp'), parts along dimension 0, may hold values from -6 to 6
- kv_grad: float32 [4, 512, 2048], P('groups', 'fsdp'), parts along dimension 0, may hold values from -12 to 12
- kv_momentum: float32 [4, 512, 2048], P('groups', 'fsdp'), parts along dimension 0, may hold values from -6 to 6
- kv_master: float32 [4, 512, 2048], P('groups', 'fsdp'), parts along dimension 0, may hold values from -6 to 6
Outputs:
- expert_master_new: float32 [8, 3, 768, 2048], P('groups', None, 'fsdp'), parts along dimension 0
- expert_momentum_new: float32 [8, 3, 768, 2048], P('groups', None, 'fsdp'), parts along dimension 0
- expert_weights: bfloat16 [8, 3, 768, 2048], P('groups', None, 'fsdp'), parts along dimension 0
- expert_update: bfloat16 [8, 3, 768, 2048], P('groups', None, 'fsdp'), parts along dimension 0
- kv_master_new: float32 [4, 512, 2048], P('groups', 'fsdp'), parts along dimension 0
- kv_momentum_new: float32 [4, 512, 2048], P('groups', 'fsdp'), parts along dimension 0
- kv_weights: bfloat16 [4, 512, 2048], P('groups', 'fsdp'), parts along dimension 0
- kv_update: bfloat16 [4, 512, 2048], P('groups', 'fsdp'), parts along dimension 0
There are 2 independent parts, one for each index of `groups`. A program takes and returns all parts, laid end to end along the dimension named above; each array names one. Nothing has to cross between parts.
All inputs are finite; a program needn't handle non-finite values.
Results may differ from a plain program's by a relative error of at most 0.014.
Values may be sent and summed in bfloat16 or wider, within the bound.
No kernel may reach another device: no remote copies, remote signals or barrier semaphores. Data moves between devices by JAX's collectives and lax.ppermute only.
A program may use at most 128 MiB of HBM per device.

v0:
```python
import functools
import math

import jax
import jax.numpy as jnp
import numpy as np
from jax import lax
from jax.experimental import pallas as pl
from jax.experimental.pallas import tpu as pltpu
from jax.sharding import PartitionSpec as P

NS_A = 3.4445
NS_B = -4.775
NS_C = 2.0315
MOMENTUM = 0.95
RATE = 0.02
DECAY = 0.1
NORM_EPS = 1e-07
CLIP_EPS = 1e-06
CLIP_RATIO = 0.5
UPDATE_GAIN = 0.2

F32 = jnp.float32
BF16 = jnp.bfloat16
VMEM_LIMIT = 40 * 1024 * 1024
LOAD_LIMIT = 42 * 1024 * 1024
STREAM_LIMIT = 16 * 1024 * 1024


def owner_table(experts, kvs, devices):
    table = np.zeros((2, devices), np.int32)
    chips = devices // 2
    first = min(experts, chips)
    for index in range(first):
        table[:, 2 * (index * chips // first)] = (1, index)
    by_parity = sorted(range(chips), key=lambda chip: bin(chip).count("1") % 2)
    for index in range(first, experts):
        table[:, 2 * by_parity[index - first] + 1] = (1, index)
    for index in range(kvs):
        low = index * devices // kvs
        free = [d for d in range(low, low + devices // kvs) if d % 2 and not table[0, d]]
        table[:, free[0]] = (2, index)
    return table


def visit_tables(table, steps):
    devices = table.shape[1]
    kinds = np.zeros((devices, len(steps)), np.int32)
    held = np.zeros((devices, len(steps)), np.int32)
    for me in range(devices):
        owners = [me ^ step for step in steps]
        experts = [table[1, owner] for owner in owners if table[0, owner] == 1]
        last = experts[0] if experts else 0
        for place, owner in enumerate(owners):
            kinds[me, place] = table[0, owner]
            last = table[1, owner] if table[0, owner] == 1 else last
            held[me, place] = last
    return kinds, held


def visits(table, steps):
    return tuple(jnp.asarray(part.reshape(-1)) for part in visit_tables(table, steps))


def fold(block, rows):
    parts = block.reshape(-1, rows, block.shape[-1])
    return jnp.sum(parts * parts, axis=0)


def load_kernel(eg, em, total, gv, mv, sems):
    chunks = sems.shape[1]
    size = gv.shape[0] // chunks
    copies = [
        [
            pltpu.make_async_copy(
                source.at[pl.ds(chunk * size, size)],
                target.at[pl.ds(chunk * size, size)],
                sems.at[place, chunk],
            )
            for chunk in range(chunks)
        ]
        for place, (source, target) in enumerate(((eg, gv), (em, mv)))
    ]
    for copy in copies[0] + copies[1]:
        copy.start()
    total[...] = jnp.zeros_like(total)
    for chunk in range(chunks):
        copies[0][chunk].wait()
        total[...] += fold(gv[chunk * size : (chunk + 1) * size], total.shape[0])
    for copy in copies[1]:
        copy.wait()


def load(eg, em):
    vmem = pl.BlockSpec(memory_space=pltpu.VMEM)
    hbm = pl.BlockSpec(memory_space=pltpu.HBM)
    chunks = eg.shape[0] // 3
    total = jax.ShapeDtypeStruct((math.gcd(8, 3 * eg.shape[1]), eg.shape[2]), F32)
    return pl.pallas_call(
        load_kernel,
        in_specs=[hbm] * 2,
        out_specs=[vmem] * 3,
        out_shape=[total] + [jax.ShapeDtypeStruct(eg.shape, F32)] * 2,
        scratch_shapes=[pltpu.SemaphoreType.DMA((2, chunks))],
        compiler_params=pltpu.CompilerParams(vmem_limit_bytes=LOAD_LIMIT),
        name="load",
    )(eg, em)


def stage_kernel(devices, me, held, total, gv, mv, kg, km, partial, staged, keep, away):
    squares = jnp.sum(total[...]) + jnp.sum(fold(kg[...], math.gcd(8, kg.shape[1])))
    partial[...] = jnp.full(partial.shape, squares, F32)
    mine = (me[0] >= devices // 2).astype(jnp.int32)
    for out, index in ((keep, mine), (away, 1 - mine)):
        out[0] = kg[index].astype(BF16)
        out[1] = km[index].astype(BF16)
    chips = staged.shape[1]
    for step in range(chips):
        expert = held[me[0] * chips + step]
        staged[0, step] = gv[expert].astype(BF16)
        staged[1, step] = mv[expert].astype(BF16)


def stage(me, table, total, gv, mv, kg, km):
    _, rows, width = gv.shape
    devices = table.shape[1]
    chips = devices // 2
    _, held = visits(table, [2 * step + 1 for step in range(chips)])
    vmem = pl.BlockSpec(memory_space=pltpu.VMEM)
    smem = pl.BlockSpec(memory_space=pltpu.SMEM)
    kv = jax.ShapeDtypeStruct((2,) + kg.shape[1:], BF16)
    return pl.pallas_call(
        functools.partial(stage_kernel, devices),
        in_specs=[smem] * 2 + [vmem] * 5,
        out_specs=[vmem] * 4,
        out_shape=[
            jax.ShapeDtypeStruct((devices, 8, 128), F32),
            jax.ShapeDtypeStruct((2, chips, rows, width), BF16),
            kv,
            kv,
        ],
        compiler_params=pltpu.CompilerParams(vmem_limit_bytes=STREAM_LIMIT),
        name="stage",
    )(me, held, total, gv, mv, kg, km)


def nesterov(scale, grad, moment):
    clipped = scale * grad.astype(F32)
    return (clipped + MOMENTUM * (MOMENTUM * moment.astype(F32) + clipped)).astype(BF16)


def form_far_kernel(count, start, me, kinds, index, squares, gv, mv, sib, clip, *outs):
    total = jnp.sum(squares[...], axis=0)
    factor = jnp.minimum(1.0, count / (jnp.sqrt(total) + CLIP_EPS))
    clip[...] = factor
    scale = factor[0:1, 0:1]
    for step, out in enumerate(outs):
        place = me[0] * len(outs) + step

        @pl.when(kinds[place] == 1)
        def _():
            out[0] = nesterov(scale, gv[index[place]], mv[index[place]])
            out[1] = nesterov(scale, sib[0, start + step], sib[1, start + step])


def form_near_kernel(
    me, kinds, index, clip, gv, mv, sib, kg, km, mirror, kv_sib, *outs
):
    scale = clip[0:1, 0:1]
    rows, kv_rows = gv.shape[1], kg.shape[1]
    mine = (me[0] >= kinds.shape[0] // len(outs) // 2).astype(jnp.int32)
    for step, out in enumerate(outs):
        place = me[0] * len(outs) + step

        @pl.when(kinds[place] == 1)
        def _():
            out[0, :rows] = nesterov(scale, gv[index[place]], mv[index[place]])
            out[1, :rows] = nesterov(scale, sib[0, step], sib[1, step])

        @pl.when(kinds[place] == 2)
        def _():
            out[0, :kv_rows] = nesterov(scale, kg[mine], km[mine])
            out[0, kv_rows : 2 * kv_rows] = nesterov(scale, mirror[0], mirror[1])
            out[1, :kv_rows] = nesterov(scale, kv_sib[0, 0], kv_sib[0, 1])
            out[1, kv_rows : 2 * kv_rows] = nesterov(scale, kv_sib[1, 0], kv_sib[1, 1])


def form_call(kernel, name, table, chip_steps, me, operands, outs):
    kinds, index = visits(table, [2 * step for step in chip_steps])
    vmem = pl.BlockSpec(memory_space=pltpu.VMEM)
    smem = pl.BlockSpec(memory_space=pltpu.SMEM)
    return pl.pallas_call(
        kernel,
        in_specs=[smem] * 3 + [vmem] * len(operands),
        out_specs=[vmem] * len(outs),
        out_shape=outs,
        compiler_params=pltpu.CompilerParams(vmem_limit_bytes=STREAM_LIMIT),
        name=name,
    )(me, kinds, index, *operands)


def form_far(me, table, steps, squares, gv, mv, sib, count):
    block = jax.ShapeDtypeStruct((2,) + gv.shape[1:], BF16)
    clip = jax.ShapeDtypeStruct((8, 128), F32)
    kernel = functools.partial(form_far_kernel, count, steps[0])
    return form_call(
        kernel, "far", table, steps, me, (squares, gv, mv, sib), [clip] + [block] * len(steps)
    )


def form_near(me, table, steps, clip, gv, mv, sib, kg, km, mirror, kv_sib):
    _, rows, width = gv.shape
    block = jax.ShapeDtypeStruct((2, max(rows, 2 * kg.shape[1]), width), BF16)
    operands = (clip, gv, mv, sib, kg, km, mirror, kv_sib)
    return form_call(
        form_near_kernel, "form", table, steps, me, operands, [block] * len(steps)
    )


def dot(left, right):
    return jnp.dot(left, right, preferred_element_type=F32)


def apply_rows(gain, x, rest, lead, low, high, store):
    width = x.shape[1]
    chunk = 512 if width % 512 == 0 else width
    for start in range(0, width, chunk):
        part = x[low:high, start : start + chunk].astype(F32)
        value = lead[low:high, 0:1] * part + dot(rest[low:high], x[:, start : start + chunk])
        value = (gain * value.astype(BF16).astype(F32)).astype(BF16)
        store(start, chunk, value)


def store_blocks(outs, rows):
    def store(start, chunk, value):
        for index, out in enumerate(outs):
            for core in range(2):
                low = (2 * index + core) * rows
                out[core, :rows, start : start + chunk] = value[low : low + rows]

    return store


def outer(left, right):
    return lax.dot_general(left, right, (((1,), (1,)), ((), ())), preferred_element_type=F32)


def transform(raw):
    size = raw.shape[0]
    row = lax.broadcasted_iota(jnp.int32, (size, size), 0)
    col = lax.broadcasted_iota(jnp.int32, (size, size), 1)
    diagonal = row == col
    norm = jnp.sqrt(jnp.sum(jnp.where(diagonal, raw, 0.0), keepdims=True))
    inverse = 1.0 / (norm + NORM_EPS)
    gram = raw * inverse * inverse
    low = gram.astype(BF16)
    first = (NS_B * low.astype(F32) + NS_C * dot(low, low)).astype(BF16)
    product = dot(first, low)
    gram = (NS_A * NS_A) * gram + (2.0 * NS_A) * product + dot(product.astype(BF16), first)
    low = gram.astype(BF16)
    second = (NS_B * low.astype(F32) + NS_C * dot(low, low)).astype(BF16)
    mixed = NS_A * (first.astype(F32) + second.astype(F32)) + dot(second, first)
    main = NS_A * NS_A + jnp.sum(jnp.where(diagonal, mixed, 0.0), axis=1, keepdims=True)
    return main * inverse, (jnp.where(diagonal, 0.0, mixed) * inverse).astype(BF16)


def place_blocks(blocks, rows, x, start):
    for index, block in enumerate(blocks):
        for core in range(2):
            low = start + (2 * index + core) * rows
            x[low : low + rows] = block[core, :rows]


def near_kernel(me, kinds, *refs):
    blocks, (x, gram) = refs[:-2], refs[-2:]

    @pl.when(kinds[me[0]] == 1)
    def _():
        place_blocks(blocks, x.shape[0] // len(blocks) // 2, x, 0)
        gram[...] = outer(x[...], x[...])


def transform_kernel(gain, kv_rows, me, kinds, near, gram, *refs):
    chips = kinds.shape[0] // 2
    kv_blocks, blocks = refs[: chips // 2], refs[chips // 2 : chips]
    (x, rest, lead), outs = refs[chips : chips + 3], refs[chips + 3 :]
    half, rows = near.shape[0], blocks[0].shape[1]
    kind = kinds[me[0]]

    @pl.when(kind == 1)
    def _():
        x[:half] = near[...]
        place_blocks(blocks, rows, x, half)
        far = x[half:]
        cross = outer(near[...], far)
        raw = jnp.concatenate(
            [
                jnp.concatenate([gram[...], cross], axis=1),
                jnp.concatenate([cross.T, outer(far, far)], axis=1),
            ],
            axis=0,
        )
        main, other = transform(raw)
        lead[...] = jnp.broadcast_to(main, lead.shape)
        rest[...] = other
        apply_rows(gain, x, rest, lead, half, 2 * half, store_blocks(outs, rows))

    @pl.when(kind == 2)
    def _():
        size = 4 * kv_rows * len(kv_blocks)
        place_blocks(kv_blocks, 2 * kv_rows, x, 0)
        main, other = transform(outer(x[:size], x[:size]))
        lead[:size] = jnp.broadcast_to(main, (size, lead.shape[1]))
        rest[:size, :size] = other


def apply_kernel(gain, kv_rows, me, kinds, x, rest, lead, *outs):
    kind = kinds[me[0]]

    @pl.when(kind == 1)
    def _():
        rows = x.shape[0] // len(outs) // 4
        apply_rows(gain, x, rest, lead, 0, x.shape[0] // 2, store_blocks(outs, rows))

    @pl.when(kind == 2)
    def _():
        size = 4 * kv_rows * len(outs)
        kv = [ref.at[:size] for ref in (x, rest, lead)]
        kv[1] = rest.at[:size, :size]
        apply_rows(gain, *kv, 0, size, store_blocks(outs, 2 * kv_rows))


def near_gram(me, kinds, blocks, rows):
    width = blocks[0].shape[2]
    half = 2 * len(blocks) * rows
    vmem = pl.BlockSpec(memory_space=pltpu.VMEM)
    smem = pl.BlockSpec(memory_space=pltpu.SMEM)
    return pl.pallas_call(
        near_kernel,
        in_specs=[smem, smem] + [vmem] * len(blocks),
        out_specs=[vmem, vmem],
        out_shape=[
            jax.ShapeDtypeStruct((half, width), BF16),
            jax.ShapeDtypeStruct((half, half), F32),
        ],
        compiler_params=pltpu.CompilerParams(vmem_limit_bytes=STREAM_LIMIT),
        cost_estimate=pl.CostEstimate(
            flops=2 * half * half * width, bytes_accessed=4 * half * width, transcendentals=0
        ),
        name="near",
    )(me, kinds, *blocks)


def orthogonal_update(me, kinds, near, gram, kv_blocks, blocks, kv_rows):
    _, rows, width = blocks[0].shape
    half = near.shape[0]
    size = 2 * half
    gain = UPDATE_GAIN * math.sqrt(width)
    vmem = pl.BlockSpec(memory_space=pltpu.VMEM)
    smem = pl.BlockSpec(memory_space=pltpu.SMEM)
    like = lambda arrays: [jax.ShapeDtypeStruct(array.shape, BF16) for array in arrays]
    params = pltpu.CompilerParams(vmem_limit_bytes=VMEM_LIMIT)
    x, rest, lead, *far = pl.pallas_call(
        functools.partial(transform_kernel, gain, kv_rows),
        in_specs=[smem, smem] + [vmem] * (2 + 2 * len(blocks)),
        out_specs=[vmem] * (3 + len(blocks)),
        out_shape=[
            jax.ShapeDtypeStruct((size, width), BF16),
            jax.ShapeDtypeStruct((size, size), BF16),
            jax.ShapeDtypeStruct((size, 128), F32),
            *like(blocks),
        ],
        compiler_params=params,
        name="transform",
    )(me, kinds, near, gram, *kv_blocks, *blocks)
    near = pl.pallas_call(
        functools.partial(apply_kernel, gain, kv_rows),
        in_specs=[smem, smem] + [vmem] * 3,
        out_specs=[vmem] * len(blocks),
        out_shape=like(kv_blocks),
        compiler_params=params,
        name="apply",
    )(me, kinds, x, rest, lead)
    return list(near), far


def gather_kernel(rows, kv_rows, me, kinds, *refs):
    if kv_rows:
        blocks, (out, kv, across) = refs[:-3], refs[-3:]
    else:
        blocks, out = refs[:-1], refs[-1]
    for index, block in enumerate(blocks):
        out[index] = block[1, :rows]
        if kv_rows:

            @pl.when(kinds[me[0] * len(blocks) + index] == 2)
            def _():
                out[len(blocks), :kv_rows] = block[1, :kv_rows]
                kv[...] = block[0, :kv_rows]
                for core in range(2):
                    across[core] = block[core, kv_rows : 2 * kv_rows]


def gather_sibling(me, table, steps, blocks, rows, kv_rows):
    width = blocks[0].shape[2]
    kinds, _ = visits(table, [2 * step for step in steps])
    vmem = pl.BlockSpec(memory_space=pltpu.VMEM)
    smem = pl.BlockSpec(memory_space=pltpu.SMEM)
    shapes = [(kv_rows, width), (2, kv_rows, width)] if kv_rows else []
    kv = [jax.ShapeDtypeStruct(shape, BF16) for shape in shapes]
    size = len(blocks) + (1 if kv_rows else 0)
    return pl.pallas_call(
        functools.partial(gather_kernel, rows, kv_rows),
        in_specs=[smem, smem] + [vmem] * len(blocks),
        out_specs=[vmem] * (1 + len(kv)),
        out_shape=[jax.ShapeDtypeStruct((size, rows, width), BF16)] + kv,
        compiler_params=pltpu.CompilerParams(vmem_limit_bytes=STREAM_LIMIT),
        name="gather",
    )(me, kinds, *blocks)


def kv_kernel(devices, me, kv, across, sibling, across_sibling, kw, ko, kb, ku):
    rows = kw.shape[1]
    mine = (me[0] >= devices // 2).astype(jnp.int32)

    def apply(index, update):
        value = kw[index] * (1.0 - RATE * DECAY) - RATE * update.astype(F32)
        ko[index] = value
        kb[index] = value.astype(BF16)
        ku[index] = update

    @pl.when(me[0] % 2 == 1)
    def _():
        apply(mine, kv[...])
        apply(1 - mine, across[0])

    @pl.when(me[0] % 2 == 0)
    def _():
        apply(mine, sibling[sibling.shape[0] - 1, :rows])
        apply(1 - mine, across_sibling[...])


def finish_kv(me, devices, sources, kw):
    vmem = pl.BlockSpec(memory_space=pltpu.VMEM)
    return pl.pallas_call(
        functools.partial(kv_kernel, devices),
        in_specs=[pl.BlockSpec(memory_space=pltpu.SMEM)] + [vmem] * 5,
        out_specs=[vmem] * 3,
        out_shape=[jax.ShapeDtypeStruct(kw.shape, kind) for kind in (F32, BF16, BF16)],
        compiler_params=pltpu.CompilerParams(vmem_limit_bytes=STREAM_LIMIT),
        name="kv",
    )(me, *sources, kw)


def finish_kernel(plan, me, kinds, held, *refs):
    own, has_sibling, has_earlier, steps, idle = plan
    owns, refs = refs[:own], list(refs[own:])
    sibling = refs.pop(0) if has_sibling else None
    ew = refs.pop(0)
    earlier, (new_ref, low_ref, update_ref) = refs[:-3], refs[-3:]
    now = pl.program_id(0)

    if has_earlier and idle:
        first = me[0] * steps
        busy = sum((kinds[first + step] == 1).astype(jnp.int32) for step in range(steps))

        @pl.when(jnp.logical_and(now == 0, busy == 0))
        def _():
            for before, after in zip(earlier, refs[-3:]):
                pltpu.sync_copy(before.at[pl.ds(held[first], 1)], after)

    def apply(update):
        value = ew[0] * (1.0 - RATE * DECAY) - RATE * update.astype(F32)
        new_ref[0] = value
        low_ref[0] = value.astype(BF16)
        update_ref[0] = update

    valid = kinds[me[0] * steps + now] == 1
    for step, block in enumerate(owns):

        @pl.when(jnp.logical_and(now == step, valid))
        def _():
            apply(block[0, : ew.shape[1]])

    if has_sibling:

        @pl.when(jnp.logical_and(now >= own, valid))
        def _():
            apply(sibling[0])


def finish(me, table, ew, owns, own_steps, sibling, sibling_steps, earlier):
    _, rows, width = ew.shape
    steps = [2 * step for step in own_steps] + [2 * step + 1 for step in sibling_steps]
    kinds, held = visits(table, steps)
    idle = not (visit_tables(table, steps)[0] == 1).any(axis=1).all()
    size, own = len(steps), len(owns)
    block = (1, rows, width)
    spec = pl.BlockSpec(block, lambda i, me, k, h: (h[me[0] * size + i], 0, 0))
    operands = [me, kinds, held, *owns]
    in_specs = [
        pl.BlockSpec((1,) + array.shape[1:], lambda i, *_: (0, 0, 0)) for array in owns
    ]
    if sibling is not None:
        last = sibling.shape[0] - 1
        in_specs.append(pl.BlockSpec(block, lambda i, *_: (jnp.clip(i - own, 0, last), 0, 0)))
        operands.append(sibling)
    in_specs.append(spec)
    operands.append(ew)
    aliases = {}
    if earlier is not None:
        aliases = {len(operands) + index: index for index in range(3)}
        in_specs += [pl.BlockSpec(memory_space=pl.ANY)] * 3
        operands += list(earlier)
    return pl.pallas_call(
        functools.partial(
            finish_kernel, (own, sibling is not None, earlier is not None, size, idle)
        ),
        grid_spec=pltpu.PrefetchScalarGridSpec(
            num_scalar_prefetch=3,
            grid=(size,),
            in_specs=in_specs,
            out_specs=[spec] * 3,
        ),
        out_shape=[jax.ShapeDtypeStruct(ew.shape, kind) for kind in (F32, BF16, BF16)],
        input_output_aliases=aliases,
        compiler_params=pltpu.CompilerParams(vmem_limit_bytes=STREAM_LIMIT),
        name="finish",
    )(*operands)


def permute(array, pairs):
    return lax.ppermute(array, "fsdp", pairs)


def together(*arrays):
    return lax.optimization_barrier(arrays)


def block_pairs(table, step, to_owners):
    devices = table.shape[1]
    kinds = (1, 2) if 2 * step < devices // 2 else (1,)
    pairs = [(d ^ (2 * step), d) for d in range(devices) if table[0, d] in kinds]
    return pairs if to_owners else [(there, here) for here, there in pairs]


def cross(blocks, table, steps, to_owners):
    moved = []
    depth = max(len(blocks) // 2, 2)
    for place, (step, block) in enumerate(zip(steps, blocks)):
        if place >= depth:
            block, moved[place - depth] = together(block, moved[place - depth])
        moved.append(permute(block, block_pairs(table, step, to_owners)))
    return moved


def shards(expert_grad, expert_momentum, expert_master, kv_grad, kv_momentum, kv_master):
    devices = lax.axis_size("fsdp")
    chips, half = devices // 2, devices // 4
    me = lax.axis_index("fsdp").reshape(1)
    shape = expert_grad.shape
    rows, width = shape[2], shape[3]
    kv_rows = kv_grad.shape[1]
    flat = lambda array: array.reshape(-1, rows, width)
    eg, em, ew = flat(expert_grad), flat(expert_momentum), flat(expert_master)
    table = owner_table(eg.shape[0], kv_grad.shape[0], devices)
    count = CLIP_RATIO * math.sqrt(devices * (expert_grad.size + kv_grad.size))
    cores = [(device, device ^ 1) for device in range(devices)]
    mirrors = [(device, device ^ chips) for device in range(devices)]
    near_steps, far_steps = list(range(half)), list(range(half, chips))

    total, gv, mv = load(eg, em)
    partial, staged, keep, away = stage(me, table, total, gv, mv, kv_grad, kv_momentum)
    mirror = permute(away, mirrors)
    squares = lax.all_to_all(partial, "fsdp", 0, 0, tiled=True)
    squares, sibling, mirror = together(squares, permute(staged, cores), mirror)

    clip, *far = form_far(me, table, far_steps, squares, gv, mv, sibling, count)
    clip, far[0], keep = together(clip, far[0], keep)
    kv_sibling = permute(jnp.stack([keep, mirror]), [pair for pair in cores if pair[1] % 2])
    near = form_near(
        me, table, near_steps, clip, gv, mv, sibling, kv_grad, kv_momentum, mirror, kv_sibling
    )
    near = list(near)
    far = cross(far, table, far_steps, True)
    for step in near_steps[1:]:
        near[step] = permute(near[step], block_pairs(table, step, True))
    kinds = jnp.asarray(table[0])

    factor = clip[0, 0]
    expert_moment_out = MOMENTUM * expert_momentum + factor * expert_grad
    kv_moment_out = MOMENTUM * kv_momentum + factor * kv_grad
    near[0], expert_moment_out, kv_moment_out = together(
        near[0], expert_moment_out, kv_moment_out
    )
    near_rows, near_product = near_gram(me, kinds, near, rows)
    near, far = orthogonal_update(me, kinds, near_rows, near_product, near, far, kv_rows)

    far = cross(far, table, far_steps, False)
    for step in near_steps[1:]:
        near[step] = permute(near[step], block_pairs(table, step, False))
    near_sibling, kv, across = gather_sibling(me, table, near_steps, near, rows, kv_rows)
    near_sibling = permute(near_sibling, cores)
    across = permute(across, [pair for pair in mirrors if pair[0] % 2])
    done = finish(me, table, ew, near, near_steps, None, [], None)
    far[0], *done = together(far[0], *done)
    across_sibling = permute(across[1], [pair for pair in cores if pair[0] % 2])
    far_sibling = permute(gather_sibling(me, table, far_steps, far, rows, 0)[0], cores)
    done = finish(me, table, ew, far, far_steps, near_sibling, near_steps, done)
    across_sibling, *done = together(across_sibling, *done)
    ko, kb, ku = finish_kv(
        me, devices, (kv, across, near_sibling, across_sibling), kv_master
    )
    eo, eb, eu = finish(me, table, ew, [], [], far_sibling, far_steps, done)
    return (
        eo.reshape(shape),
        expert_moment_out,
        eb.reshape(shape),
        eu.reshape(shape),
        ko,
        kv_moment_out,
        kb,
        ku,
    )


def solution(mesh):
    expert = P("groups", None, "fsdp", None)
    kv = P("groups", "fsdp", None)
    return jax.shard_map(
        shards,
        mesh=mesh,
        in_specs=(expert, expert, expert, kv, kv, kv),
        out_specs=(expert, expert, expert, expert, kv, kv, kv, kv),
        check_vma=False,
    )
```

profile of v0, /device:TPU:1, one launch (start us, length us, event | category | flops | bytes accessed | tf_op | source)
XLA Modules:
  0.0 174.1 jit_solution(12649198563245575254)
XLA Ops:
  0.7 3.9 %load.1 = (f32[8,2048]{1,0:T(8,128)S(1)}, f32[12,48,2048]{2,1,0:T(8,128)S(1)}, f32[12,48,2048]{2,1,0:T(8,128)S(1)}) custom-call(f32[12,48,2048]{2,1,0:T(8,128)} %bitcast.20, f32[12,48,2048]{2,1,0:T(8,128)} %bitcast.23), custom_call_target="tpu_custom_call" | custom-call | tf_op jit(solution)/shard_map/load/pallas_call | solution.py:99
  5.7 3.8 %collective-permute-start.1 = (bf16[2,32,2048]{2,1,0:T(8,128)(2,1)S(1)}, bf16[2,32,2048]{2,1,0:T(8,128)(2,1)S(1)}, u32[]{:S(2)}, u32[]{:S(2)}) collective-permute-start(bf16[2,32,2048]{2,1,0:T(8,128)(2,1)S(1)} %get-tuple-element.82), channel_id=1, source_target_pairs={{0,8},{1,9},{2,10},{3,11},{4,12},{5,13},{6,14},{7,15},{8,0},{9,1},... | collective-permute-start | bytes 786440 | tf_op jit(solution)/shard_map/ppermute | solution.py:533
  9.5 14.6 %all_to_all.5.squares = f32[16,8,128]{2,1,0:T(8,128)S(1)} all-to-all(f32[16,8,128]{2,1,0:T(8,128)S(1)} %get-tuple-element.80), channel_id=1, replica_groups=mesh['groups'=2,'fsdp'=16] {'fsdp'}, dimensions={0} | all-to-all | bytes 131072 | tf_op jit(solution)/shard_map/all_to_all | solution.py:575
  26.7 4.2 %collective-permute-start.7 = (bf16[2,48,2048]{2,1,0:T(8,128)(2,1)S(1)}, bf16[2,48,2048]{2,1,0:T(8,128)(2,1)S(1)}, u32[]{:S(2)}, u32[]{:S(2)}) collective-permute-start(bf16[2,48,2048]{2,1,0:T(8,128)(2,1)S(1)} %get-tuple-element.102), channel_id=1, source_target_pairs={{10,0},{11,1},{8,2},{14,4},{12,6},{13,7},{2,8},{0,10},{1,11},{6,12... | collective-permute-start | bytes 1179656 | tf_op jit(solution)/shard_map/ppermute | solution.py:533
  32.8 1.6 form.1
  34.4 3.9 %collective-permute-start.3 = (bf16[2,64,2048]{2,1,0:T(8,128)(2,1)S(1)}, bf16[2,64,2048]{2,1,0:T(8,128)(2,1)S(1)}, u32[]{:S(2)}, u32[]{:S(2)}) collective-permute-start(bf16[2,64,2048]{2,1,0:T(8,128)(2,1)S(1)} %get-tuple-element.93), channel_id=1, source_target_pairs={{2,0},{3,1},{0,2},{1,3},{6,4},{4,6},{5,7},{10,8},{11,9},{8,10},{9,... | collective-permute-start | bytes 1572872 | tf_op jit(solution)/shard_map/ppermute | solution.py:533
  39.6 3.7 %collective-permute-start.5 = (bf16[2,64,2048]{2,1,0:T(8,128)(2,1)S(1)}, bf16[2,64,2048]{2,1,0:T(8,128)(2,1)S(1)}, u32[]{:S(2)}, u32[]{:S(2)}) collective-permute-start(bf16[2,64,2048]{2,1,0:T(8,128)(2,1)S(1)} %get-tuple-element.95), channel_id=1, source_target_pairs={{6,0},{7,1},{4,2},{5,3},{2,4},{0,6},{1,7},{14,8},{15,9},{12,10},{1... | collective-permute-start | bytes 1572872 | tf_op jit(solution)/shard_map/ppermute | solution.py:533
  43.4 4.3 %multiply_add_fusion = f32[4,3,48,2048]{3,2,1,0:T(8,128)} fusion(f32[4,3,48,2048]{3,2,1,0:T(8,128)S(1)} %bitcast.22, f32[4,3,48,2048]{3,2,1,0:T(8,128)S(1)} %bitcast.25, f32[]{:T(128)} %bitcast.5), kind=kLoop, calls=%fused_computation | loop fusion | flops 3538944 | bytes 14155780 | tf_op jit(solution)/shard_map/add | solution.py:591
  47.7 4.8 %collective-permute-done.7.refs_5_ = bf16[2,48,2048]{2,1,0:T(8,128)(2,1)S(1)} collective-permute-done((bf16[2,48,2048]{2,1,0:T(8,128)(2,1)S(1)}, bf16[2,48,2048]{2,1,0:T(8,128)(2,1)S(1)}, u32[]{:S(2)}, u32[]{:S(2)}) %collective-permute-start.7) | collective-permute-done | bytes 393248 | tf_op jit(solution)/shard_map/ppermute | solution.py:533
  54.3 4.6 %collective-permute-start.8 = (bf16[2,48,2048]{2,1,0:T(8,128)(2,1)S(1)}, bf16[2,48,2048]{2,1,0:T(8,128)(2,1)S(1)}, u32[]{:S(2)}, u32[]{:S(2)}) collective-permute-start(bf16[2,48,2048]{2,1,0:T(8,128)(2,1)S(1)} %get-tuple-element.104), channel_id=1, source_target_pairs={{12,0},{13,1},{14,2},{8,4},{10,6},{11,7},{4,8},{6,10},{7,11},{0,12... | collective-permute-start | bytes 1179656 | tf_op jit(solution)/shard_map/ppermute | solution.py:533
  59.0 1.5 multiply_add_fusion.1
  60.5 4.2 %collective-permute-done.4.refs_2_ = bf16[2,64,2048]{2,1,0:T(8,128)(2,1)S(1)} collective-permute-done((bf16[2,64,2048]{2,1,0:T(8,128)(2,1)S(1)}, bf16[2,64,2048]{2,1,0:T(8,128)(2,1)S(1)}, u32[]{:S(2)}, u32[]{:S(2)}) %collective-permute-start.4) | collective-permute-done | bytes 524320 | tf_op jit(solution)/shard_map/ppermute | solution.py:533
  64.7 20.8 %collective-permute-done.5.refs_3_ = bf16[2,64,2048]{2,1,0:T(8,128)(2,1)S(1)} collective-permute-done((bf16[2,64,2048]{2,1,0:T(8,128)(2,1)S(1)}, bf16[2,64,2048]{2,1,0:T(8,128)(2,1)S(1)}, u32[]{:S(2)}, u32[]{:S(2)}) %collective-permute-start.5) | collective-permute-done | bytes 524320 | tf_op jit(solution)/shard_map/ppermute | solution.py:533
  85.5 1.6 near.1
  87.1 9.4 %transform.1 = (bf16[768,2048]{1,0:T(8,128)(2,1)S(1)}, bf16[768,768]{1,0:T(8,128)(2,1)S(1)}, f32[768,128]{1,0:T(8,128)S(1)}, bf16[2,48,2048]{2,1,0:T(8,128)(2,1)...) custom-call(s32[1]{0:T(128)} %bitcast.me, ...), custom_call_target="tpu_custom_call" | custom-call | tf_op jit(solution)/shard_map/transform/pallas_call | solution.py:363
  96.5 1.9 %collective-permute-start.14 = (bf16[2,48,2048]{2,1,0:T(8,128)(2,1)S(1)}, bf16[2,48,2048]{2,1,0:T(8,128)(2,1)S(1)}, u32[]{:S(2)}, u32[]{:S(2)}) collective-permute-start(bf16[2,48,2048]{2,1,0:T(8,128)(2,1)S(1)} %get-tuple-element.121), channel_id=1, source_target_pairs={{0,10},{1,11},{2,8},{4,14},{6,12},{7,13},{8,2},{10,0},{11,1},{12,6... | collective-permute-start | bytes 1179656 | tf_op jit(solution)/shard_map/ppermute | solution.py:533
  98.4 1.3 collective-permute-start.10
  99.8 2.0 %apply.1 = (bf16[2,64,2048]{2,1,0:T(8,128)(2,1)S(1)}, bf16[2,64,2048]{2,1,0:T(8,128)(2,1)S(1)}, bf16[2,64,2048]{2,1,0:T(8,128)(2,1)S(1)}, bf16[2,64,2048]{2,1,0:T(8,128)(2,1)S(1)}) custom-call(s32[1]{0:T(128)} %bitcast.me, s32[16]{0:T(128)S(1)} %copy-done.5, bf16[768,2048]{1,0:T(8,128)(2,1)S(1)} %get-tuple-element.109.x, ...), custom_call_target="tpu_custom_call" | custom-call | tf_op jit(solution)/shard_map/apply/pallas_call | solution.py:376
  101.8 2.1 %collective-permute-start.11 = (bf16[2,64,2048]{2,1,0:T(8,128)(2,1)S(1)}, bf16[2,64,2048]{2,1,0:T(8,128)(2,1)S(1)}, u32[]{:S(2)}, u32[]{:S(2)}) collective-permute-start(bf16[2,64,2048]{2,1,0:T(8,128)(2,1)S(1)} %get-tuple-element.113), channel_id=1, source_target_pairs={{0,2},{1,3},{2,0},{3,1},{4,6},{6,4},{7,5},{8,10},{9,11},{10,8},{11... | collective-permute-start | bytes 1572872 | tf_op jit(solution)/shard_map/ppermute | solution.py:533
  104.0 1.3 collective-permute-start.12
  105.3 5.1 %collective-permute-start.13 = (bf16[2,64,2048]{2,1,0:T(8,128)(2,1)S(1)}, bf16[2,64,2048]{2,1,0:T(8,128)(2,1)S(1)}, u32[]{:S(2)}, u32[]{:S(2)}) collective-permute-start(bf16[2,64,2048]{2,1,0:T(8,128)(2,1)S(1)} %get-tuple-element.115), channel_id=1, source_target_pairs={{0,6},{1,7},{2,4},{3,5},{4,2},{6,0},{7,1},{8,14},{9,15},{10,12},{1... | collective-permute-start | bytes 1572872 | tf_op jit(solution)/shard_map/ppermute | solution.py:533
  112.1 3.7 %collective-permute-start.15 = (bf16[2,48,2048]{2,1,0:T(8,128)(2,1)S(1)}, bf16[2,48,2048]{2,1,0:T(8,128)(2,1)S(1)}, u32[]{:S(2)}, u32[]{:S(2)}) collective-permute-start(bf16[2,48,2048]{2,1,0:T(8,128)(2,1)S(1)} %get-tuple-element.123), channel_id=1, source_target_pairs={{0,12},{1,13},{2,14},{4,8},{6,10},{7,11},{8,4},{10,6},{11,7},{12,0... | collective-permute-start | bytes 1179656 | tf_op jit(solution)/shard_map/ppermute | solution.py:533
  115.8 7.6 %collective-permute-done.12.refs_2_ = bf16[2,64,2048]{2,1,0:T(8,128)(2,1)S(1)} collective-permute-done((bf16[2,64,2048]{2,1,0:T(8,128)(2,1)S(1)}, bf16[2,64,2048]{2,1,0:T(8,128)(2,1)S(1)}, u32[]{:S(2)}, u32[]{:S(2)}) %collective-permute-start.12) | collective-permute-done | bytes 524320 | tf_op jit(solution)/shard_map/ppermute | solution.py:533
  123.4 22.1 %collective-permute-done.13.refs_3_ = bf16[2,64,2048]{2,1,0:T(8,128)(2,1)S(1)} collective-permute-done((bf16[2,64,2048]{2,1,0:T(8,128)(2,1)S(1)}, bf16[2,64,2048]{2,1,0:T(8,128)(2,1)S(1)}, u32[]{:S(2)}, u32[]{:S(2)}) %collective-permute-start.13) | collective-permute-done | bytes 524320 | tf_op jit(solution)/shard_map/ppermute | solution.py:533
  146.1 7.5 %collective-permute-start.20 = (bf16[5,48,2048]{2,1,0:T(8,128)(2,1)S(1)}, bf16[5,48,2048]{2,1,0:T(8,128)(2,1)S(1)}, u32[]{:S(2)}, u32[]{:S(2)}) collective-permute-start(bf16[5,48,2048]{2,1,0:T(8,128)(2,1)S(1)} %get-tuple-element.126), channel_id=1, source_target_pairs={{0,1},{1,0},{2,3},{3,2},{4,5},{5,4},{6,7},{7,6},{8,9},{9,8},{10,11... | collective-permute-start | bytes 2949128 | tf_op jit(solution)/shard_map/ppermute | solution.py:533
  153.6 1.9 %collective-permute-start.18 = (bf16[2,32,2048]{2,1,0:T(8,128)(2,1)S(1)}, bf16[2,32,2048]{2,1,0:T(8,128)(2,1)S(1)}, u32[]{:S(2)}, u32[]{:S(2)}) collective-permute-start(bf16[2,32,2048]{2,1,0:T(8,128)(2,1)S(1)} %get-tuple-element.125), channel_id=1, source_target_pairs={{1,9},{3,11},{5,13},{7,15},{9,1},{11,3},{13,5},{15,7},{17,25},{19,... | collective-permute-start | bytes 786440 | tf_op jit(solution)/shard_map/ppermute | solution.py:533
  155.5 2.0 %finish.3 = (f32[12,48,2048]{2,1,0:T(8,128)}, bf16[12,48,2048]{2,1,0:T(8,128)(2,1)}, bf16[12,48,2048]{2,1,0:T(8,128)(2,1)}) custom-call(s32[1]{0:T(128)} %bitcast.me, s32[64]{0:T(128)S(1)} %copy-done.3, s32[64]{0:T(128)S(1)} %copy-done.4, bf16[2,64,2048]{2,1,0:T(8,128)(2,1)S(1)} %get-tuple-element.112.refs_0_, ...), custom_call_target="tpu_custom_call" | custom-call | tf_op jit(solution)/shard_map/finish/pallas_call | solution.py:515
  158.2 4.7 %collective-permute-start.17 = (bf16[4,48,2048]{2,1,0:T(8,128)(2,1)S(1)}, bf16[4,48,2048]{2,1,0:T(8,128)(2,1)S(1)}, u32[]{:S(2)}, u32[]{:S(2)}) collective-permute-start(bf16[4,48,2048]{2,1,0:T(8,128)(2,1)S(1)} %gather.2), channel_id=1, source_target_pairs={{0,1},{1,0},{2,3},{3,2},{4,5},{5,4},{6,7},{7,6},{8,9},{9,8},{10,11... | collective-permute-start | bytes 2359304 | tf_op jit(solution)/shard_map/ppermute | solution.py:533
  162.9 1.4 collective-permute-done.18.across
  164.3 1.4 collective-permute-start.19
  165.8 4.5 %finish.4 = (f32[12,48,2048]{2,1,0:T(8,128)}, bf16[12,48,2048]{2,1,0:T(8,128)(2,1)}, bf16[12,48,2048]{2,1,0:T(8,128)(2,1)}) custom-call(s32[1]{0:T(128)} %bitcast.me, s32[128]{0:T(128)S(1)} %copy-done.9, s32[128]{0:T(128)S(1)} %copy-done.10, ...), custom_call_target="tpu_custom_call", output_to_operand_aliasing={{0}: (9, {}), {1}: (10, {}), {2}: (11, {})} | custom-call | tf_op jit(solution)/shard_map/finish/pallas_call | solution.py:515
  171.3 2.8 %finish.5 = (f32[12,48,2048]{2,1,0:T(8,128)}, bf16[12,48,2048]{2,1,0:T(8,128)(2,1)}, bf16[12,48,2048]{2,1,0:T(8,128)(2,1)}) custom-call(s32[1]{0:T(128)} %bitcast.me, s32[64]{0:T(128)S(1)} %copy-done.7, s32[64]{0:T(128)S(1)} %copy-done.8, ...), custom_call_target="tpu_custom_call", output_to_operand_aliasing={{0}: (5, {}), {1}: (6, {}), {2}: (7, {})} | custom-call | tf_op jit(solution)/shard_map/finish/pallas_call | solution.py:515
  (70 shorter events, 12.7 us)
Async XLA Ops:
  4.6 19.5 %copy-start.6 = (s32[64]{0:T(128)S(1)}, s32[64]{0:T(128)}, u32[]{:S(2)}) copy-start(s32[64]{0:T(128)} %constant.28.clone.kinds) | copy-start | bytes 772
  4.6 19.5 %copy-start.11 = (s32[64]{0:T(128)S(1)}, s32[64]{0:T(128)}, u32[]{:S(2)}) copy-start(s32[64]{0:T(128)} %constant.29.clone.index) | copy-start | bytes 772
  5.6 18.5 %collective-permute-start = (bf16[2,8,48,2048]{3,2,1,0:T(8,128)(2,1)S(1)}, bf16[2,8,48,2048]{3,2,1,0:T(8,128)(2,1)S(1)}, u32[]{:S(2)}, u32[]{:S(2)}) collective-permute-start(bf16[2,8,48,2048]{3,2,1,0:T(8,128)(2,1)S(1)} %get-tuple-element.81), channel_id=1, source_target_pairs={{0,1},{1,0},{2,3},{3,2},{4,5},{5,4},{6,7},{7,6},{8,9},{9,8},{10,11... | collective-permute-start | bytes 9437192 | tf_op jit(solution)/shard_map/ppermute | solution.py:533
  5.7 18.4 %collective-permute-start.1 = (bf16[2,32,2048]{2,1,0:T(8,128)(2,1)S(1)}, bf16[2,32,2048]{2,1,0:T(8,128)(2,1)S(1)}, u32[]{:S(2)}, u32[]{:S(2)}) collective-permute-start(bf16[2,32,2048]{2,1,0:T(8,128)(2,1)S(1)} %get-tuple-element.82), channel_id=1, source_target_pairs={{0,8},{1,9},{2,10},{3,11},{4,12},{5,13},{6,14},{7,15},{8,0},{9,1},... | collective-permute-start | bytes 786440 | tf_op jit(solution)/shard_map/ppermute | solution.py:533
  25.4 7.4 %collective-permute-start.2 = (bf16[2,2,32,2048]{3,2,1,0:T(8,128)(2,1)S(1)}, bf16[2,2,32,2048]{3,2,1,0:T(8,128)(2,1)S(1)}, u32[]{:S(2)}, u32[]{:S(2)}) collective-permute-start(bf16[2,2,32,2048]{3,2,1,0:T(8,128)(2,1)S(1)} %pad_maximum_fusion), channel_id=1, source_target_pairs={{0,1},{2,3},{4,5},{6,7},{8,9},{10,11},{12,13},{14,15},{16,17},{18,... | collective-permute-start | bytes 1572872 | tf_op jit(solution)/shard_map/ppermute | solution.py:533
  26.7 25.8 %collective-permute-start.7 = (bf16[2,48,2048]{2,1,0:T(8,128)(2,1)S(1)}, bf16[2,48,2048]{2,1,0:T(8,128)(2,1)S(1)}, u32[]{:S(2)}, u32[]{:S(2)}) collective-permute-start(bf16[2,48,2048]{2,1,0:T(8,128)(2,1)S(1)} %get-tuple-element.102), channel_id=1, source_target_pairs={{10,0},{11,1},{8,2},{14,4},{12,6},{13,7},{2,8},{0,10},{1,11},{6,12... | collective-permute-start | bytes 1179656 | tf_op jit(solution)/shard_map/ppermute | solution.py:533
  30.9 23.4 %collective-permute-start.6 = (bf16[2,48,2048]{2,1,0:T(8,128)(2,1)S(1)}, bf16[2,48,2048]{2,1,0:T(8,128)(2,1)S(1)}, u32[]{:S(2)}, u32[]{:S(2)}) collective-permute-start(bf16[2,48,2048]{2,1,0:T(8,128)(2,1)S(1)} %get-tuple-element.99), channel_id=1, source_target_pairs={{8,0},{9,1},{10,2},{12,4},{14,6},{15,7},{0,8},{2,10},{3,11},{4,12}... | collective-permute-start | bytes 1179656 | tf_op jit(solution)/shard_map/ppermute | solution.py:533
  32.2 11.1 %slice-start.2 = ((s8[4718592]{0:T(1024)(128)(4,1)}), s8[4194304]{0:T(1024)(128)(4,1)S(1)}, s32[]{:S(2)}) async-start(s8[4718592]{0:T(1024)(128)(4,1)} %bitcast.21), calls=%async_computation.3 | async-start | bytes 8388608
  32.2 11.1 %slice-start.4 = ((s8[4718592]{0:T(1024)(128)(4,1)}), s8[4194304]{0:T(1024)(128)(4,1)S(1)}, s32[]{:S(2)}) async-start(s8[4718592]{0:T(1024)(128)(4,1)} %bitcast.24), calls=%async_computation.5 | async-start | bytes 8388608
  32.8 10.5 %slice-start.3 = ((s8[4718592]{0:T(1024)(128)(4,1)}), s8[524288]{0:T(1024)(128)(4,1)S(1)}, s32[]{:S(2)}) async-start(s8[4718592]{0:T(1024)(128)(4,1)} %bitcast.21), calls=%async_computation.4 | async-start | bytes 1048576
  32.8 10.5 %slice-start.5 = ((s8[4718592]{0:T(1024)(128)(4,1)}), s8[524288]{0:T(1024)(128)(4,1)S(1)}, s32[]{:S(2)}) async-start(s8[4718592]{0:T(1024)(128)(4,1)} %bitcast.24), calls=%async_computation.6 | async-start | bytes 1048576
  34.4 26.1 %collective-permute-start.3 = (bf16[2,64,2048]{2,1,0:T(8,128)(2,1)S(1)}, bf16[2,64,2048]{2,1,0:T(8,128)(2,1)S(1)}, u32[]{:S(2)}, u32[]{:S(2)}) collective-permute-start(bf16[2,64,2048]{2,1,0:T(8,128)(2,1)S(1)} %get-tuple-element.93), channel_id=1, source_target_pairs={{2,0},{3,1},{0,2},{1,3},{6,4},{4,6},{5,7},{10,8},{11,9},{8,10},{9,... | collective-permute-start | bytes 1572872 | tf_op jit(solution)/shard_map/ppermute | solution.py:533
  38.3 26.4 %collective-permute-start.4 = (bf16[2,64,2048]{2,1,0:T(8,128)(2,1)S(1)}, bf16[2,64,2048]{2,1,0:T(8,128)(2,1)S(1)}, u32[]{:S(2)}, u32[]{:S(2)}) collective-permute-start(bf16[2,64,2048]{2,1,0:T(8,128)(2,1)S(1)} %get-tuple-element.94), channel_id=1, source_target_pairs={{4,0},{5,1},{6,2},{7,3},{0,4},{2,6},{3,7},{12,8},{13,9},{14,10},{1... | collective-permute-start | bytes 1572872 | tf_op jit(solution)/shard_map/ppermute | solution.py:533
  39.6 45.9 %collective-permute-start.5 = (bf16[2,64,2048]{2,1,0:T(8,128)(2,1)S(1)}, bf16[2,64,2048]{2,1,0:T(8,128)(2,1)S(1)}, u32[]{:S(2)}, u32[]{:S(2)}) collective-permute-start(bf16[2,64,2048]{2,1,0:T(8,128)(2,1)S(1)} %get-tuple-element.95), channel_id=1, source_target_pairs={{6,0},{7,1},{4,2},{5,3},{2,4},{0,6},{1,7},{14,8},{15,9},{12,10},{1... | collective-permute-start | bytes 1572872 | tf_op jit(solution)/shard_map/ppermute | solution.py:533
  43.3 42.1 %copy-start.5 = (s32[16]{0:T(128)S(1)}, s32[16]{0:T(128)}, u32[]{:S(2)}) copy-start(s32[16]{0:T(128)} %constant.32.clone.kinds) | copy-start | bytes 196
  52.5 34.5 %collective-permute-start.9 = (bf16[2,48,2048]{2,1,0:T(8,128)(2,1)S(1)}, bf16[2,48,2048]{2,1,0:T(8,128)(2,1)S(1)}, u32[]{:S(2)}, u32[]{:S(2)}) collective-permute-start(bf16[2,48,2048]{2,1,0:T(8,128)(2,1)S(1)} %get-tuple-element.105), channel_id=1, source_target_pairs={{14,0},{15,1},{12,2},{10,4},{8,6},{9,7},{6,8},{4,10},{5,11},{2,12}... | collective-permute-start | bytes 1179656 | tf_op jit(solution)/shard_map/ppermute | solution.py:533
  54.3 32.7 %collective-permute-start.8 = (bf16[2,48,2048]{2,1,0:T(8,128)(2,1)S(1)}, bf16[2,48,2048]{2,1,0:T(8,128)(2,1)S(1)}, u32[]{:S(2)}, u32[]{:S(2)}) collective-permute-start(bf16[2,48,2048]{2,1,0:T(8,128)(2,1)S(1)} %get-tuple-element.104), channel_id=1, source_target_pairs={{12,0},{13,1},{14,2},{8,4},{10,6},{11,7},{4,8},{6,10},{7,11},{0,12... | collective-permute-start | bytes 1179656 | tf_op jit(solution)/shard_map/ppermute | solution.py:533
  85.5 70.0 %slice-start = ((s8[4718592]{0:T(1024)(128)(4,1)}), s8[4194304]{0:T(1024)(128)(4,1)S(1)}, s32[]{:S(2)}) async-start(s8[4718592]{0:T(1024)(128)(4,1)} %bitcast.12), calls=%async_computation.1 | async-start | bytes 8388608
  87.1 68.5 %slice-start.1 = ((s8[4718592]{0:T(1024)(128)(4,1)}), s8[524288]{0:T(1024)(128)(4,1)S(1)}, s32[]{:S(2)}) async-start(s8[4718592]{0:T(1024)(128)(4,1)} %bitcast.12), calls=%async_computation.2 | async-start | bytes 1048576
  96.5 13.9 %collective-permute-start.14 = (bf16[2,48,2048]{2,1,0:T(8,128)(2,1)S(1)}, bf16[2,48,2048]{2,1,0:T(8,128)(2,1)S(1)}, u32[]{:S(2)}, u32[]{:S(2)}) collective-permute-start(bf16[2,48,2048]{2,1,0:T(8,128)(2,1)S(1)} %get-tuple-element.121), channel_id=1, source_target_pairs={{0,10},{1,11},{2,8},{4,14},{6,12},{7,13},{8,2},{10,0},{11,1},{12,6... | collective-permute-start | bytes 1179656 | tf_op jit(solution)/shard_map/ppermute | solution.py:533
  98.4 13.7 %collective-permute-start.10 = (bf16[2,48,2048]{2,1,0:T(8,128)(2,1)S(1)}, bf16[2,48,2048]{2,1,0:T(8,128)(2,1)S(1)}, u32[]{:S(2)}, u32[]{:S(2)}) collective-permute-start(bf16[2,48,2048]{2,1,0:T(8,128)(2,1)S(1)} %get-tuple-element.107), channel_id=1, source_target_pairs={{0,8},{1,9},{2,10},{4,12},{6,14},{7,15},{8,0},{10,2},{11,3},{12,4}... | collective-permute-start | bytes 1179656 | tf_op jit(solution)/shard_map/ppermute | solution.py:533
  101.8 14.0 %collective-permute-start.11 = (bf16[2,64,2048]{2,1,0:T(8,128)(2,1)S(1)}, bf16[2,64,2048]{2,1,0:T(8,128)(2,1)S(1)}, u32[]{:S(2)}, u32[]{:S(2)}) collective-permute-start(bf16[2,64,2048]{2,1,0:T(8,128)(2,1)S(1)} %get-tuple-element.113), channel_id=1, source_target_pairs={{0,2},{1,3},{2,0},{3,1},{4,6},{6,4},{7,5},{8,10},{9,11},{10,8},{11... | collective-permute-start | bytes 1572872 | tf_op jit(solution)/shard_map/ppermute | solution.py:533
  104.0 19.4 %collective-permute-start.12 = (bf16[2,64,2048]{2,1,0:T(8,128)(2,1)S(1)}, bf16[2,64,2048]{2,1,0:T(8,128)(2,1)S(1)}, u32[]{:S(2)}, u32[]{:S(2)}) collective-permute-start(bf16[2,64,2048]{2,1,0:T(8,128)(2,1)S(1)} %get-tuple-element.114), channel_id=1, source_target_pairs={{0,4},{1,5},{2,6},{3,7},{4,0},{6,2},{7,3},{8,12},{9,13},{10,14},{1... | collective-permute-start | bytes 1572872 | tf_op jit(solution)/shard_map/ppermute | solution.py:533
  105.3 40.2 %collective-permute-start.13 = (bf16[2,64,2048]{2,1,0:T(8,128)(2,1)S(1)}, bf16[2,64,2048]{2,1,0:T(8,128)(2,1)S(1)}, u32[]{:S(2)}, u32[]{:S(2)}) collective-permute-start(bf16[2,64,2048]{2,1,0:T(8,128)(2,1)S(1)} %get-tuple-element.115), channel_id=1, source_target_pairs={{0,6},{1,7},{2,4},{3,5},{4,2},{6,0},{7,1},{8,14},{9,15},{10,12},{1... | collective-permute-start | bytes 1572872 | tf_op jit(solution)/shard_map/ppermute | solution.py:533
  110.4 47.1 %collective-permute-start.16 = (bf16[2,48,2048]{2,1,0:T(8,128)(2,1)S(1)}, bf16[2,48,2048]{2,1,0:T(8,128)(2,1)S(1)}, u32[]{:S(2)}, u32[]{:S(2)}) collective-permute-start(bf16[2,48,2048]{2,1,0:T(8,128)(2,1)S(1)} %get-tuple-element.124), channel_id=1, source_target_pairs={{0,14},{1,15},{2,12},{4,10},{6,8},{7,9},{8,6},{10,4},{11,5},{12,2}... | collective-permute-start | bytes 1179656 | tf_op jit(solution)/shard_map/ppermute | solution.py:533
  112.1 45.4 %collective-permute-start.15 = (bf16[2,48,2048]{2,1,0:T(8,128)(2,1)S(1)}, bf16[2,48,2048]{2,1,0:T(8,128)(2,1)S(1)}, u32[]{:S(2)}, u32[]{:S(2)}) collective-permute-start(bf16[2,48,2048]{2,1,0:T(8,128)(2,1)S(1)} %get-tuple-element.123), channel_id=1, source_target_pairs={{0,12},{1,13},{2,14},{4,8},{6,10},{7,11},{8,4},{10,6},{11,7},{12,0... | collective-permute-start | bytes 1179656 | tf_op jit(solution)/shard_map/ppermute | solution.py:533
  146.1 19.6 %collective-permute-start.20 = (bf16[5,48,2048]{2,1,0:T(8,128)(2,1)S(1)}, bf16[5,48,2048]{2,1,0:T(8,128)(2,1)S(1)}, u32[]{:S(2)}, u32[]{:S(2)}) collective-permute-start(bf16[5,48,2048]{2,1,0:T(8,128)(2,1)S(1)} %get-tuple-element.126), channel_id=1, source_target_pairs={{0,1},{1,0},{2,3},{3,2},{4,5},{5,4},{6,7},{7,6},{8,9},{9,8},{10,11... | collective-permute-start | bytes 2949128 | tf_op jit(solution)/shard_map/ppermute | solution.py:533
  153.6 10.7 %collective-permute-start.18 = (bf16[2,32,2048]{2,1,0:T(8,128)(2,1)S(1)}, bf16[2,32,2048]{2,1,0:T(8,128)(2,1)S(1)}, u32[]{:S(2)}, u32[]{:S(2)}) collective-permute-start(bf16[2,32,2048]{2,1,0:T(8,128)(2,1)S(1)} %get-tuple-element.125), channel_id=1, source_target_pairs={{1,9},{3,11},{5,13},{7,15},{9,1},{11,3},{13,5},{15,7},{17,25},{19,... | collective-permute-start | bytes 786440 | tf_op jit(solution)/shard_map/ppermute | solution.py:533
  155.5 10.2 %copy-start.9 = (s32[128]{0:T(128)S(1)}, s32[128]{0:T(128)}, u32[]{:S(2)}) copy-start(s32[128]{0:T(128)} %constant.33.clone.kinds) | copy-start | bytes 1540
  155.5 10.2 %copy-start.10 = (s32[128]{0:T(128)S(1)}, s32[128]{0:T(128)}, u32[]{:S(2)}) copy-start(s32[128]{0:T(128)} %constant.34.clone.held) | copy-start | bytes 1540
  158.2 13.1 %collective-permute-start.17 = (bf16[4,48,2048]{2,1,0:T(8,128)(2,1)S(1)}, bf16[4,48,2048]{2,1,0:T(8,128)(2,1)S(1)}, u32[]{:S(2)}, u32[]{:S(2)}) collective-permute-start(bf16[4,48,2048]{2,1,0:T(8,128)(2,1)S(1)} %gather.2), channel_id=1, source_target_pairs={{0,1},{1,0},{2,3},{3,2},{4,5},{5,4},{6,7},{7,6},{8,9},{9,8},{10,11... | collective-permute-start | bytes 2359304 | tf_op jit(solution)/shard_map/ppermute | solution.py:533
  164.3 5.9 %collective-permute-start.19 = (bf16[32,2048]{1,0:T(8,128)(2,1)S(1)}, bf16[32,2048]{1,0:T(8,128)(2,1)S(1)}, u32[]{:S(2)}, u32[]{:S(2)}) collective-permute-start(bf16[32,2048]{1,0:T(8,128)(2,1)S(1)} %slice_bitcast_fusion), channel_id=1, source_target_pairs={{1,0},{3,2},{5,4},{7,6},{9,8},{11,10},{13,12},{15,14},{17,16},{19,... | collective-permute-start | bytes 393224 | tf_op jit(solution)/shard_map/ppermute | solution.py:533
  (8 other events, 49.3 us)
where the time goes:
time: 175 us; the launch traced here: 174 us
  waiting for transfers between devices  61.8 us (35%)
  starting transfers between devices  57.9 us (33%)
  Pallas kernels  32.2 us (18%)
  blocking collectives  14.6 us (8%)
  other arithmetic  5.89 us (3%)
    ppermute x21, waiting for transfers between devices, permute(): return lax.ppermute(array, 'fsdp', pairs)  61.8 us
    ppermute x21, starting transfers between devices, permute(): return lax.ppermute(array, 'fsdp', pairs)  57.9 us
    all_to_all x1, blocking collectives, shards(): squares = lax.all_to_all(partial, 'fsdp', 0, 0, tiled=True)  14.6 us
    pallas_call x1, Pallas kernels, orthogonal_update(): pl.pallas_call(functools.partial(transform_kernel, gain, kv_rows), in_spe...  9.44 us
    pallas_call x3, Pallas kernels, finish(): pl.pallas_call(functools.partial(finish_kernel, (own, sibling is not None...  9.24 us
    add x1, other arithmetic, shards(): expert_moment_out = MOMENTUM * expert_momentum + factor * expert_grad  4.34 us
    pallas_call x1, Pallas kernels, load(): pl.pallas_call(load_kernel, in_specs=[hbm] * 2, out_specs=[vmem] * 3, out...  3.86 us
  transfers between devices with their start and end apart: 21, of which 8 were waited for; matrix products, arithmetic and copies ran while one was open for 4% of the time, Pallas kernels for 8%

commit v1 on v0

--- a/solution.py
+++ b/solution.py
@@ -163,26 +163,24 @@
             out[1] = nesterov(scale, sib[0, start + step], sib[1, start + step])
 
 
-def form_near_kernel(
-    me, kinds, index, clip, gv, mv, sib, kg, km, mirror, kv_sib, *outs
-):
+def form_near_kernel(me, kinds, index, clip, gv, mv, sib, kg, km, mirror, kv_sib, *outs):
     scale = clip[0:1, 0:1]
-    rows, kv_rows = gv.shape[1], kg.shape[1]
-    mine = (me[0] >= kinds.shape[0] // len(outs) // 2).astype(jnp.int32)
-    for step, out in enumerate(outs):
-        place = me[0] * len(outs) + step
+    steps, kv_rows = len(outs) // 2, kg.shape[1]
+    mine = (me[0] >= kinds.shape[0] // steps // 2).astype(jnp.int32)
+    for step, (out, kv) in enumerate(zip(outs[:steps], outs[steps:])):
+        place = me[0] * steps + step
 
         @pl.when(kinds[place] == 1)
         def _():
-            out[0, :rows] = nesterov(scale, gv[index[place]], mv[index[place]])
-            out[1, :rows] = nesterov(scale, sib[0, step], sib[1, step])
+            out[0] = nesterov(scale, gv[index[place]], mv[index[place]])
+            out[1] = nesterov(scale, sib[0, step], sib[1, step])
 
         @pl.when(kinds[place] == 2)
         def _():
-            out[0, :kv_rows] = nesterov(scale, kg[mine], km[mine])
-            out[0, kv_rows : 2 * kv_rows] = nesterov(scale, mirror[0], mirror[1])
-            out[1, :kv_rows] = nesterov(scale, kv_sib[0, 0], kv_sib[0, 1])
-            out[1, kv_rows : 2 * kv_rows] = nesterov(scale, kv_sib[1, 0], kv_sib[1, 1])
+            kv[0, :kv_rows] = nesterov(scale, kg[mine], km[mine])
+            kv[0, kv_rows:] = nesterov(scale, mirror[0], mirror[1])
+            kv[1, :kv_rows] = nesterov(scale, kv_sib[0, 0], kv_sib[0, 1])
+            kv[1, kv_rows:] = nesterov(scale, kv_sib[1, 0], kv_sib[1, 1])
 
 
 def form_call(kernel, name, table, chip_steps, me, operands, outs):
@@ -210,11 +208,11 @@
 
 def form_near(me, table, steps, clip, gv, mv, sib, kg, km, mirror, kv_sib):
     _, rows, width = gv.shape
-    block = jax.ShapeDtypeStruct((2, max(rows, 2 * kg.shape[1]), width), BF16)
+    shapes = [(2, rows, width)] * len(steps) + [(2, 2 * kg.shape[1], width)] * len(steps)
+    outs = [jax.ShapeDtypeStruct(shape, BF16) for shape in shapes]
     operands = (clip, gv, mv, sib, kg, km, mirror, kv_sib)
-    return form_call(
-        form_near_kernel, "form", table, steps, me, operands, [block] * len(steps)
-    )
+    blocks = form_call(form_near_kernel, "form", table, steps, me, operands, outs)
+    return list(blocks[: len(steps)]), list(blocks[len(steps) :])
 
 
 def dot(left, right):
@@ -303,7 +301,8 @@
         main, other = transform(raw)
         lead[...] = jnp.broadcast_to(main, lead.shape)
         rest[...] = other
-        apply_rows(gain, x, rest, lead, half, 2 * half, store_blocks(outs, rows))
+        high = half + 2 * rows * len(outs)
+        apply_rows(gain, x, rest, lead, half, high, store_blocks(outs, rows))
 
     @pl.when(kind == 2)
     def _():
@@ -314,20 +313,22 @@
         rest[:size, :size] = other
 
 
-def apply_kernel(gain, kv_rows, me, kinds, x, rest, lead, *outs):
+def apply_kernel(gain, rows, kv_rows, me, kinds, x, rest, lead, *outs):
+    steps = kinds.shape[0] // 4
+    near, far = outs[:steps], outs[steps:]
     kind = kinds[me[0]]
 
     @pl.when(kind == 1)
     def _():
-        rows = x.shape[0] // len(outs) // 4
-        apply_rows(gain, x, rest, lead, 0, x.shape[0] // 2, store_blocks(outs, rows))
+        apply_rows(gain, x, rest, lead, 0, x.shape[0] // 2, store_blocks(near, rows))
+        low = x.shape[0] - 2 * rows * len(far)
+        apply_rows(gain, x, rest, lead, low, x.shape[0], store_blocks(far, rows))
 
     @pl.when(kind == 2)
     def _():
-        size = 4 * kv_rows * len(outs)
-        kv = [ref.at[:size] for ref in (x, rest, lead)]
-        kv[1] = rest.at[:size, :size]
-        apply_rows(gain, *kv, 0, size, store_blocks(outs, 2 * kv_rows))
+        size = 4 * kv_rows * steps
+        part = x.at[:size], rest.at[:size, :size], lead.at[:size]
+        apply_rows(gain, *part, 0, size, store_blocks(near, 2 * kv_rows))
 
 
 def near_gram(me, kinds, blocks, rows):
@@ -360,28 +361,32 @@
     smem = pl.BlockSpec(memory_space=pltpu.SMEM)
     like = lambda arrays: [jax.ShapeDtypeStruct(array.shape, BF16) for array in arrays]
     params = pltpu.CompilerParams(vmem_limit_bytes=VMEM_LIMIT)
+    early = max(len(blocks) // 2, 1)
     x, rest, lead, *far = pl.pallas_call(
         functools.partial(transform_kernel, gain, kv_rows),
         in_specs=[smem, smem] + [vmem] * (2 + 2 * len(blocks)),
-        out_specs=[vmem] * (3 + len(blocks)),
+        out_specs=[vmem] * (3 + early),
         out_shape=[
             jax.ShapeDtypeStruct((size, width), BF16),
             jax.ShapeDtypeStruct((size, size), BF16),
             jax.ShapeDtypeStruct((size, 128), F32),
-            *like(blocks),
+            *like(blocks[:early]),
         ],
         compiler_params=params,
         name="transform",
     )(me, kinds, near, gram, *kv_blocks, *blocks)
-    near = pl.pallas_call(
-        functools.partial(apply_kernel, gain, kv_rows),
+    slot = (2, max(rows, 2 * kv_rows), width)
+    outs = [jax.ShapeDtypeStruct(slot, BF16)] * len(blocks) + like(blocks[early:])
+    outs = pl.pallas_call(
+        functools.partial(apply_kernel, gain, rows, kv_rows),
         in_specs=[smem, smem] + [vmem] * 3,
-        out_specs=[vmem] * len(blocks),
-        out_shape=like(kv_blocks),
+        out_specs=[vmem] * len(outs),
+        out_shape=outs,
         compiler_params=params,
         name="apply",
     )(me, kinds, x, rest, lead)
-    return list(near), far
+    steps = len(blocks)
+    return list(outs[:steps]), far + list(outs[steps:])
 
 
 def gather_kernel(rows, kv_rows, me, kinds, *refs):
@@ -537,9 +542,8 @@
     return lax.optimization_barrier(arrays)
 
 
-def block_pairs(table, step, to_owners):
+def block_pairs(table, step, to_owners, kinds=(1,)):
     devices = table.shape[1]
-    kinds = (1, 2) if 2 * step < devices // 2 else (1,)
     pairs = [(d ^ (2 * step), d) for d in range(devices) if table[0, d] in kinds]
     return pairs if to_owners else [(there, here) for here, there in pairs]
 
@@ -578,13 +582,13 @@
     clip, *far = form_far(me, table, far_steps, squares, gv, mv, sibling, count)
     clip, far[0], keep = together(clip, far[0], keep)
     kv_sibling = permute(jnp.stack([keep, mirror]), [pair for pair in cores if pair[1] % 2])
-    near = form_near(
+    near, kv = form_near(
         me, table, near_steps, clip, gv, mv, sibling, kv_grad, kv_momentum, mirror, kv_sibling
     )
-    near = list(near)
     far = cross(far, table, far_steps, True)
     for step in near_steps[1:]:
         near[step] = permute(near[step], block_pairs(table, step, True))
+        kv[step] = permute(kv[step], block_pairs(table, step, True, (2,)))
     kinds = jnp.asarray(table[0])
 
     factor = clip[0, 0]
@@ -594,11 +598,11 @@
         near[0], expert_moment_out, kv_moment_out
     )
     near_rows, near_product = near_gram(me, kinds, near, rows)
-    near, far = orthogonal_update(me, kinds, near_rows, near_product, near, far, kv_rows)
+    near, far = orthogonal_update(me, kinds, near_rows, near_product, kv, far, kv_rows)
 
     far = cross(far, table, far_steps, False)
     for step in near_steps[1:]:
-        near[step] = permute(near[step], block_pairs(table, step, False))
+        near[step] = permute(near[step], block_pairs(table, step, False, (1, 2)))
     near_sibling, kv, across = gather_sibling(me, table, near_steps, near, rows, kv_rows)
     near_sibling = permute(near_sibling, cores)
     across = permute(across, [pair for pair in mirrors if pair[0] % 2])

time: 175 us -> 171 us (0.977)
  waiting for transfers between devices: 61.8 us -> 30.8 us
  starting transfers between devices: 57.9 us -> 84.6 us
    ppermute x21 -> x24, waiting for transfers between devices: 61.8 us -> 30.8 us  [permute(): return lax.ppermute(array, 'fsdp', pairs)]
    ppermute x21 -> x24, starting transfers between devices: 57.9 us -> 84.6 us  [permute(): return lax.ppermute(array, 'fsdp', pairs)]
  transfers between devices with their start and end apart: 21 -> 24, of which waited for: 8 -> 7; matrix products, arithmetic and copies ran while one was open for 4% -> 4% of each run, Pallas kernels for 8% -> 9%
where the time goes in v1:
time: 171 us; the launch traced here: 170 us
  starting transfers between devices  84.6 us (49%)
  Pallas kernels  32.6 us (19%)
  waiting for transfers between devices  30.8 us (18%)
  blocking collectives  14.6 us (9%)
  other arithmetic  5.89 us (3%)
    ppermute x24, starting transfers between devices, permute(): return lax.ppermute(array, 'fsdp', pairs)  84.6 us
    ppermute x24, waiting for transfers between devices, permute(): return lax.ppermute(array, 'fsdp', pairs)  30.8 us
    all_to_all x1, blocking collectives, shards(): squares = lax.all_to_all(partial, 'fsdp', 0, 0, tiled=True)  14.6 us
    pallas_call x3, Pallas kernels, finish(): pl.pallas_call(functools.partial(finish_kernel, (own, sibling is not None...  9.24 us
    pallas_call x1, Pallas kernels, orthogonal_update(): pl.pallas_call(functools.partial(transform_kernel, gain, kv_rows), in_spe...  8.93 us
    add x1, other arithmetic, shards(): expert_moment_out = MOMENTUM * expert_momentum + factor * expert_grad  4.34 us
    pallas_call x1, Pallas kernels, load(): pl.pallas_call(load_kernel, in_specs=[hbm] * 2, out_specs=[vmem] * 3, out...  3.86 us
  transfers between devices with their start and end apart: 24, of which 7 were waited for; matrix products, arithmetic and copies ran while one was open for 4% of the time, Pallas kernels for 9%

profile of v1, /device:TPU:1, one launch (start us, length us, event | category | flops | bytes accessed | tf_op | source)
XLA Modules:
  0.0 170.3 jit_solution(10262934328636225522)
XLA Ops:
  0.7 3.9 %load.1 = (f32[8,2048]{1,0:T(8,128)S(1)}, f32[12,48,2048]{2,1,0:T(8,128)S(1)}, f32[12,48,2048]{2,1,0:T(8,128)S(1)}) custom-call(f32[12,48,2048]{2,1,0:T(8,128)} %bitcast.20, f32[12,48,2048]{2,1,0:T(8,128)} %bitcast.23), custom_call_target="tpu_custom_call" | custom-call | tf_op jit(solution)/shard_map/load/pallas_call | solution.py:99
  5.7 3.8 %collective-permute-start.1 = (bf16[2,32,2048]{2,1,0:T(8,128)(2,1)S(1)}, bf16[2,32,2048]{2,1,0:T(8,128)(2,1)S(1)}, u32[]{:S(2)}, u32[]{:S(2)}) collective-permute-start(bf16[2,32,2048]{2,1,0:T(8,128)(2,1)S(1)} %get-tuple-element.86), channel_id=1, source_target_pairs={{0,8},{1,9},{2,10},{3,11},{4,12},{5,13},{6,14},{7,15},{8,0},{9,1},... | collective-permute-start | bytes 786440 | tf_op jit(solution)/shard_map/ppermute | solution.py:538
  9.5 14.6 %all_to_all.5.squares = f32[16,8,128]{2,1,0:T(8,128)S(1)} all-to-all(f32[16,8,128]{2,1,0:T(8,128)S(1)} %get-tuple-element.84), channel_id=1, replica_groups=mesh['groups'=2,'fsdp'=16] {'fsdp'}, dimensions={0} | all-to-all | bytes 131072 | tf_op jit(solution)/shard_map/all_to_all | solution.py:579
  26.7 4.2 %collective-permute-start.10 = (bf16[2,48,2048]{2,1,0:T(8,128)(2,1)S(1)}, bf16[2,48,2048]{2,1,0:T(8,128)(2,1)S(1)}, u32[]{:S(2)}, u32[]{:S(2)}) collective-permute-start(bf16[2,48,2048]{2,1,0:T(8,128)(2,1)S(1)} %get-tuple-element.110), channel_id=1, source_target_pairs={{10,0},{11,1},{8,2},{14,4},{12,6},{13,7},{2,8},{0,10},{1,11},{6,12... | collective-permute-start | bytes 1179656 | tf_op jit(solution)/shard_map/ppermute | solution.py:538
  30.9 1.3 collective-permute-start.9
  32.8 1.6 form.1
  34.4 1.4 collective-permute-start.3
  37.1 4.0 %collective-permute-start.5 = (bf16[2,48,2048]{2,1,0:T(8,128)(2,1)S(1)}, bf16[2,48,2048]{2,1,0:T(8,128)(2,1)S(1)}, u32[]{:S(2)}, u32[]{:S(2)}) collective-permute-start(bf16[2,48,2048]{2,1,0:T(8,128)(2,1)S(1)} %get-tuple-element.99), channel_id=1, source_target_pairs={{6,0},{7,1},{4,2},{2,4},{0,6},{1,7},{14,8},{12,10},{13,11},{10,12}... | collective-permute-start | bytes 1179656 | tf_op jit(solution)/shard_map/ppermute | solution.py:538
  41.2 4.3 %multiply_add_fusion = f32[4,3,48,2048]{3,2,1,0:T(8,128)} fusion(f32[4,3,48,2048]{3,2,1,0:T(8,128)S(1)} %bitcast.22, f32[4,3,48,2048]{3,2,1,0:T(8,128)S(1)} %bitcast.25, f32[]{:T(128)} %bitcast.5), kind=kLoop, calls=%fused_computation | loop fusion | flops 3538944 | bytes 14155780 | tf_op jit(solution)/shard_map/add | solution.py:595
  45.6 6.9 %collective-permute-done.10.refs_5_ = bf16[2,48,2048]{2,1,0:T(8,128)(2,1)S(1)} collective-permute-done((bf16[2,48,2048]{2,1,0:T(8,128)(2,1)S(1)}, bf16[2,48,2048]{2,1,0:T(8,128)(2,1)S(1)}, u32[]{:S(2)}, u32[]{:S(2)}) %collective-permute-start.10) | collective-permute-done | bytes 393248 | tf_op jit(solution)/shard_map/ppermute | solution.py:538
  54.3 4.6 %collective-permute-start.11 = (bf16[2,48,2048]{2,1,0:T(8,128)(2,1)S(1)}, bf16[2,48,2048]{2,1,0:T(8,128)(2,1)S(1)}, u32[]{:S(2)}, u32[]{:S(2)}) collective-permute-start(bf16[2,48,2048]{2,1,0:T(8,128)(2,1)S(1)} %get-tuple-element.112), channel_id=1, source_target_pairs={{12,0},{13,1},{14,2},{8,4},{10,6},{11,7},{4,8},{6,10},{7,11},{0,12... | collective-permute-start | bytes 1179656 | tf_op jit(solution)/shard_map/ppermute | solution.py:538
  59.0 2.5 %collective-permute-start.6 = (bf16[2,64,2048]{2,1,0:T(8,128)(2,1)S(1)}, bf16[2,64,2048]{2,1,0:T(8,128)(2,1)S(1)}, u32[]{:S(2)}, u32[]{:S(2)}) collective-permute-start(bf16[2,64,2048]{2,1,0:T(8,128)(2,1)S(1)} %get-tuple-element.103), channel_id=1, source_target_pairs={{1,3},{11,9},{17,19},{27,25}} | collective-permute-start | bytes 1572872 | tf_op jit(solution)/shard_map/ppermute | solution.py:538
  63.0 1.5 multiply_add_fusion.1
  64.5 1.5 near.1
  66.2 1.3 collective-permute-done.11.refs_6_
  67.6 9.6 %collective-permute-done.6.refs_1_ = bf16[2,64,2048]{2,1,0:T(8,128)(2,1)S(1)} collective-permute-done((bf16[2,64,2048]{2,1,0:T(8,128)(2,1)S(1)}, bf16[2,64,2048]{2,1,0:T(8,128)(2,1)S(1)}, u32[]{:S(2)}, u32[]{:S(2)}) %collective-permute-start.6) | collective-permute-done | bytes 524320 | tf_op jit(solution)/shard_map/ppermute | solution.py:538
  77.2 8.9 %transform.1 = (bf16[768,2048]{1,0:T(8,128)(2,1)S(1)}, bf16[768,768]{1,0:T(8,128)(2,1)S(1)}, f32[768,128]{1,0:T(8,128)S(1)}, bf16[2,48,2048]{2,1,0:T(8,128)(2,1)S(1)}, bf16[2,48,2048]{2,1,0:T(8,128)(2,1)S(1)}) custom-call(s32[1]{0:T(128)} %bitcast.me, s32[16]{0:T(128)S(1)} %copy-done.5, bf16[384,2048]{1,0:T(8,128)(2,1)S(1)} %get-tuple-element.100.near, ...), custom_call_target="tpu_custom_call" | custom-call | tf_op jit(solution)/shard_map/transform/pallas_call | solution.py:365
  86.1 4.8 %collective-permute-start.17 = (bf16[2,48,2048]{2,1,0:T(8,128)(2,1)S(1)}, bf16[2,48,2048]{2,1,0:T(8,128)(2,1)S(1)}, u32[]{:S(2)}, u32[]{:S(2)}) collective-permute-start(bf16[2,48,2048]{2,1,0:T(8,128)(2,1)S(1)} %get-tuple-element.129), channel_id=1, source_target_pairs={{0,10},{1,11},{2,8},{4,14},{6,12},{7,13},{8,2},{10,0},{11,1},{12,6... | collective-permute-start | bytes 1179656 | tf_op jit(solution)/shard_map/ppermute | solution.py:538
  90.9 1.3 collective-permute-start.13
  92.2 2.9 %apply.1 = (bf16[2,64,2048]{2,1,0:T(8,128)(2,1)S(1)}, bf16[2,64,2048]{2,1,0:T(8,128)(2,1)S(1)}, bf16[2,64,2048]{2,1,0:T(8,128)(2,1)S(1)}, bf16[2,64,2048]{2,1,0:...) custom-call(s32[1]{0:T(128)} %bitcast.me, s32[16]{0:T(128)S(1)} %copy-done.5, ...), custom_call_target="tpu_custom_call" | custom-call | tf_op jit(solution)/shard_map/apply/pallas_call | solution.py:380
  95.2 1.9 %collective-permute-start.14 = (bf16[2,64,2048]{2,1,0:T(8,128)(2,1)S(1)}, bf16[2,64,2048]{2,1,0:T(8,128)(2,1)S(1)}, u32[]{:S(2)}, u32[]{:S(2)}) collective-permute-start(bf16[2,64,2048]{2,1,0:T(8,128)(2,1)S(1)} %get-tuple-element.121), channel_id=1, source_target_pairs={{0,2},{1,3},{2,0},{3,1},{4,6},{6,4},{7,5},{8,10},{9,11},{10,8},{11... | collective-permute-start | bytes 1572872 | tf_op jit(solution)/shard_map/ppermute | solution.py:538
  97.1 1.3 collective-permute-start.15
  98.4 5.3 %collective-permute-start.16 = (bf16[2,64,2048]{2,1,0:T(8,128)(2,1)S(1)}, bf16[2,64,2048]{2,1,0:T(8,128)(2,1)S(1)}, u32[]{:S(2)}, u32[]{:S(2)}) collective-permute-start(bf16[2,64,2048]{2,1,0:T(8,128)(2,1)S(1)} %get-tuple-element.123), channel_id=1, source_target_pairs={{0,6},{1,7},{2,4},{3,5},{4,2},{6,0},{7,1},{8,14},{9,15},{10,12},{1... | collective-permute-start | bytes 1572872 | tf_op jit(solution)/shard_map/ppermute | solution.py:538
  103.8 1.3 collective-permute-start.19
  105.1 5.6 %collective-permute-start.18 = (bf16[2,48,2048]{2,1,0:T(8,128)(2,1)S(1)}, bf16[2,48,2048]{2,1,0:T(8,128)(2,1)S(1)}, u32[]{:S(2)}, u32[]{:S(2)}) collective-permute-start(bf16[2,48,2048]{2,1,0:T(8,128)(2,1)S(1)} %get-tuple-element.131), channel_id=1, source_target_pairs={{0,12},{1,13},{2,14},{4,8},{6,10},{7,11},{8,4},{10,6},{11,7},{12,0... | collective-permute-start | bytes 1179656 | tf_op jit(solution)/shard_map/ppermute | solution.py:538
  110.8 11.1 %collective-permute-done.16.refs_3_ = bf16[2,64,2048]{2,1,0:T(8,128)(2,1)S(1)} collective-permute-done((bf16[2,64,2048]{2,1,0:T(8,128)(2,1)S(1)}, bf16[2,64,2048]{2,1,0:T(8,128)(2,1)S(1)}, u32[]{:S(2)}, u32[]{:S(2)}) %collective-permute-start.16) | collective-permute-done | bytes 524320 | tf_op jit(solution)/shard_map/ppermute | solution.py:538
  122.6 21.2 %collective-permute-start.23 = (bf16[5,48,2048]{2,1,0:T(8,128)(2,1)S(1)}, bf16[5,48,2048]{2,1,0:T(8,128)(2,1)S(1)}, u32[]{:S(2)}, u32[]{:S(2)}) collective-permute-start(bf16[5,48,2048]{2,1,0:T(8,128)(2,1)S(1)} %get-tuple-element.134), channel_id=1, source_target_pairs={{0,1},{1,0},{2,3},{3,2},{4,5},{5,4},{6,7},{7,6},{8,9},{9,8},{10,11... | collective-permute-start | bytes 2949128 | tf_op jit(solution)/shard_map/ppermute | solution.py:538
  143.8 12.9 %collective-permute-start.21 = (bf16[2,32,2048]{2,1,0:T(8,128)(2,1)S(1)}, bf16[2,32,2048]{2,1,0:T(8,128)(2,1)S(1)}, u32[]{:S(2)}, u32[]{:S(2)}) collective-permute-start(bf16[2,32,2048]{2,1,0:T(8,128)(2,1)S(1)} %get-tuple-element.133), channel_id=1, source_target_pairs={{1,9},{3,11},{5,13},{7,15},{9,1},{11,3},{13,5},{15,7},{17,25},{19,... | collective-permute-start | bytes 786440 | tf_op jit(solution)/shard_map/ppermute | solution.py:538
  156.7 2.0 %finish.3 = (f32[12,48,2048]{2,1,0:T(8,128)}, bf16[12,48,2048]{2,1,0:T(8,128)(2,1)}, bf16[12,48,2048]{2,1,0:T(8,128)(2,1)}) custom-call(s32[1]{0:T(128)} %bitcast.me, s32[64]{0:T(128)S(1)} %copy-done.3, s32[64]{0:T(128)S(1)} %copy-done.4, bf16[2,64,2048]{2,1,0:T(8,128)(2,1)S(1)} %get-tuple-element.120.refs_0_, ...), custom_call_target="tpu_custom_call" | custom-call | tf_op jit(solution)/shard_map/finish/pallas_call | solution.py:520
  160.4 1.5 collective-permute-start.22
  162.0 4.5 %finish.4 = (f32[12,48,2048]{2,1,0:T(8,128)}, bf16[12,48,2048]{2,1,0:T(8,128)(2,1)}, bf16[12,48,2048]{2,1,0:T(8,128)(2,1)}) custom-call(s32[1]{0:T(128)} %bitcast.me, s32[128]{0:T(128)S(1)} %copy-done.9, s32[128]{0:T(128)S(1)} %copy-done.10, ...), custom_call_target="tpu_custom_call", output_to_operand_aliasing={{0}: (9, {}), {1}: (10, {}), {2}: (11, {})} | custom-call | tf_op jit(solution)/shard_map/finish/pallas_call | solution.py:520
  167.6 2.8 %finish.5 = (f32[12,48,2048]{2,1,0:T(8,128)}, bf16[12,48,2048]{2,1,0:T(8,128)(2,1)}, bf16[12,48,2048]{2,1,0:T(8,128)(2,1)}) custom-call(s32[1]{0:T(128)} %bitcast.me, s32[64]{0:T(128)S(1)} %copy-done.7, s32[64]{0:T(128)S(1)} %copy-done.8, ...), custom_call_target="tpu_custom_call", output_to_operand_aliasing={{0}: (5, {}), {1}: (6, {}), {2}: (7, {})} | custom-call | tf_op jit(solution)/shard_map/finish/pallas_call | solution.py:520
  (76 shorter events, 12.5 us)
Async XLA Ops:
  4.6 19.5 %copy-start.6 = (s32[64]{0:T(128)S(1)}, s32[64]{0:T(128)}, u32[]{:S(2)}) copy-start(s32[64]{0:T(128)} %constant.28.clone.kinds) | copy-start | bytes 772
  4.6 19.5 %copy-start.11 = (s32[64]{0:T(128)S(1)}, s32[64]{0:T(128)}, u32[]{:S(2)}) copy-start(s32[64]{0:T(128)} %constant.29.clone.index) | copy-start | bytes 772
  5.6 18.5 %collective-permute-start = (bf16[2,8,48,2048]{3,2,1,0:T(8,128)(2,1)S(1)}, bf16[2,8,48,2048]{3,2,1,0:T(8,128)(2,1)S(1)}, u32[]{:S(2)}, u32[]{:S(2)}) collective-permute-start(bf16[2,8,48,2048]{3,2,1,0:T(8,128)(2,1)S(1)} %get-tuple-element.85), channel_id=1, source_target_pairs={{0,1},{1,0},{2,3},{3,2},{4,5},{5,4},{6,7},{7,6},{8,9},{9,8},{10,11... | collective-permute-start | bytes 9437192 | tf_op jit(solution)/shard_map/ppermute | solution.py:538
  5.7 18.4 %collective-permute-start.1 = (bf16[2,32,2048]{2,1,0:T(8,128)(2,1)S(1)}, bf16[2,32,2048]{2,1,0:T(8,128)(2,1)S(1)}, u32[]{:S(2)}, u32[]{:S(2)}) collective-permute-start(bf16[2,32,2048]{2,1,0:T(8,128)(2,1)S(1)} %get-tuple-element.86), channel_id=1, source_target_pairs={{0,8},{1,9},{2,10},{3,11},{4,12},{5,13},{6,14},{7,15},{8,0},{9,1},... | collective-permute-start | bytes 786440 | tf_op jit(solution)/shard_map/ppermute | solution.py:538
  24.1 8.7 %copy-start.4 = (s32[64]{0:T(128)S(1)}, s32[64]{0:T(128)}, u32[]{:S(2)}) copy-start(s32[64]{0:T(128)} %constant.31.clone.index.held) | copy-start | bytes 772
  25.4 7.4 %collective-permute-start.2 = (bf16[2,2,32,2048]{3,2,1,0:T(8,128)(2,1)S(1)}, bf16[2,2,32,2048]{3,2,1,0:T(8,128)(2,1)S(1)}, u32[]{:S(2)}, u32[]{:S(2)}) collective-permute-start(bf16[2,2,32,2048]{3,2,1,0:T(8,128)(2,1)S(1)} %pad_maximum_fusion), channel_id=1, source_target_pairs={{0,1},{2,3},{4,5},{6,7},{8,9},{10,11},{12,13},{14,15},{16,17},{18,... | collective-permute-start | bytes 1572872 | tf_op jit(solution)/shard_map/ppermute | solution.py:538
  26.7 25.8 %collective-permute-start.10 = (bf16[2,48,2048]{2,1,0:T(8,128)(2,1)S(1)}, bf16[2,48,2048]{2,1,0:T(8,128)(2,1)S(1)}, u32[]{:S(2)}, u32[]{:S(2)}) collective-permute-start(bf16[2,48,2048]{2,1,0:T(8,128)(2,1)S(1)} %get-tuple-element.110), channel_id=1, source_target_pairs={{10,0},{11,1},{8,2},{14,4},{12,6},{13,7},{2,8},{0,10},{1,11},{6,12... | collective-permute-start | bytes 1179656 | tf_op jit(solution)/shard_map/ppermute | solution.py:538
  30.9 23.4 %collective-permute-start.9 = (bf16[2,48,2048]{2,1,0:T(8,128)(2,1)S(1)}, bf16[2,48,2048]{2,1,0:T(8,128)(2,1)S(1)}, u32[]{:S(2)}, u32[]{:S(2)}) collective-permute-start(bf16[2,48,2048]{2,1,0:T(8,128)(2,1)S(1)} %get-tuple-element.107), channel_id=1, source_target_pairs={{8,0},{9,1},{10,2},{12,4},{14,6},{15,7},{0,8},{2,10},{3,11},{4,12}... | collective-permute-start | bytes 1179656 | tf_op jit(solution)/shard_map/ppermute | solution.py:538
  32.2 8.9 %slice-start.2 = ((s8[4718592]{0:T(1024)(128)(4,1)}), s8[4194304]{0:T(1024)(128)(4,1)S(1)}, s32[]{:S(2)}) async-start(s8[4718592]{0:T(1024)(128)(4,1)} %bitcast.21), calls=%async_computation.3 | async-start | bytes 8388608
  32.2 8.9 %slice-start.4 = ((s8[4718592]{0:T(1024)(128)(4,1)}), s8[4194304]{0:T(1024)(128)(4,1)S(1)}, s32[]{:S(2)}) async-start(s8[4718592]{0:T(1024)(128)(4,1)} %bitcast.24), calls=%async_computation.5 | async-start | bytes 8388608
  34.4 24.6 %collective-permute-start.3 = (bf16[2,48,2048]{2,1,0:T(8,128)(2,1)S(1)}, bf16[2,48,2048]{2,1,0:T(8,128)(2,1)S(1)}, u32[]{:S(2)}, u32[]{:S(2)}) collective-permute-start(bf16[2,48,2048]{2,1,0:T(8,128)(2,1)S(1)} %get-tuple-element.97), channel_id=1, source_target_pairs={{2,0},{3,1},{0,2},{6,4},{4,6},{5,7},{10,8},{8,10},{9,11},{14,12},{... | collective-permute-start | bytes 1179656 | tf_op jit(solution)/shard_map/ppermute | solution.py:538
  35.8 25.7 %collective-permute-start.4 = (bf16[2,48,2048]{2,1,0:T(8,128)(2,1)S(1)}, bf16[2,48,2048]{2,1,0:T(8,128)(2,1)S(1)}, u32[]{:S(2)}, u32[]{:S(2)}) collective-permute-start(bf16[2,48,2048]{2,1,0:T(8,128)(2,1)S(1)} %get-tuple-element.98), channel_id=1, source_target_pairs={{4,0},{5,1},{6,2},{0,4},{2,6},{3,7},{12,8},{14,10},{15,11},{8,12},... | collective-permute-start | bytes 1179656 | tf_op jit(solution)/shard_map/ppermute | solution.py:538
  37.1 25.1 %collective-permute-start.5 = (bf16[2,48,2048]{2,1,0:T(8,128)(2,1)S(1)}, bf16[2,48,2048]{2,1,0:T(8,128)(2,1)S(1)}, u32[]{:S(2)}, u32[]{:S(2)}) collective-permute-start(bf16[2,48,2048]{2,1,0:T(8,128)(2,1)S(1)} %get-tuple-element.99), channel_id=1, source_target_pairs={{6,0},{7,1},{4,2},{2,4},{0,6},{1,7},{14,8},{12,10},{13,11},{10,12}... | collective-permute-start | bytes 1179656 | tf_op jit(solution)/shard_map/ppermute | solution.py:538
  41.2 23.2 %copy-start.5 = (s32[16]{0:T(128)S(1)}, s32[16]{0:T(128)}, u32[]{:S(2)}) copy-start(s32[16]{0:T(128)} %constant.32.clone.kinds) | copy-start | bytes 196
  52.5 13.7 %collective-permute-start.12 = (bf16[2,48,2048]{2,1,0:T(8,128)(2,1)S(1)}, bf16[2,48,2048]{2,1,0:T(8,128)(2,1)S(1)}, u32[]{:S(2)}, u32[]{:S(2)}) collective-permute-start(bf16[2,48,2048]{2,1,0:T(8,128)(2,1)S(1)} %get-tuple-element.113), channel_id=1, source_target_pairs={{14,0},{15,1},{12,2},{10,4},{8,6},{9,7},{6,8},{4,10},{5,11},{2,12}... | collective-permute-start | bytes 1179656 | tf_op jit(solution)/shard_map/ppermute | solution.py:538
  54.3 13.2 %collective-permute-start.11 = (bf16[2,48,2048]{2,1,0:T(8,128)(2,1)S(1)}, bf16[2,48,2048]{2,1,0:T(8,128)(2,1)S(1)}, u32[]{:S(2)}, u32[]{:S(2)}) collective-permute-start(bf16[2,48,2048]{2,1,0:T(8,128)(2,1)S(1)} %get-tuple-element.112), channel_id=1, source_target_pairs={{12,0},{13,1},{14,2},{8,4},{10,6},{11,7},{4,8},{6,10},{7,11},{0,12... | collective-permute-start | bytes 1179656 | tf_op jit(solution)/shard_map/ppermute | solution.py:538
  59.0 18.2 %collective-permute-start.6 = (bf16[2,64,2048]{2,1,0:T(8,128)(2,1)S(1)}, bf16[2,64,2048]{2,1,0:T(8,128)(2,1)S(1)}, u32[]{:S(2)}, u32[]{:S(2)}) collective-permute-start(bf16[2,64,2048]{2,1,0:T(8,128)(2,1)S(1)} %get-tuple-element.103), channel_id=1, source_target_pairs={{1,3},{11,9},{17,19},{27,25}} | collective-permute-start | bytes 1572872 | tf_op jit(solution)/shard_map/ppermute | solution.py:538
  61.5 15.7 %collective-permute-start.7 = (bf16[2,64,2048]{2,1,0:T(8,128)(2,1)S(1)}, bf16[2,64,2048]{2,1,0:T(8,128)(2,1)S(1)}, u32[]{:S(2)}, u32[]{:S(2)}) collective-permute-start(bf16[2,64,2048]{2,1,0:T(8,128)(2,1)S(1)} %get-tuple-element.104), channel_id=1, source_target_pairs={{7,3},{13,9},{23,19},{29,25}} | collective-permute-start | bytes 1572872 | tf_op jit(solution)/shard_map/ppermute | solution.py:538
  62.2 15.0 %collective-permute-start.8 = (bf16[2,64,2048]{2,1,0:T(8,128)(2,1)S(1)}, bf16[2,64,2048]{2,1,0:T(8,128)(2,1)S(1)}, u32[]{:S(2)}, u32[]{:S(2)}) collective-permute-start(bf16[2,64,2048]{2,1,0:T(8,128)(2,1)S(1)} %get-tuple-element.105), channel_id=1, source_target_pairs={{5,3},{15,9},{21,19},{31,25}} | collective-permute-start | bytes 1572872 | tf_op jit(solution)/shard_map/ppermute | solution.py:538
  64.5 92.2 %slice-start = ((s8[4718592]{0:T(1024)(128)(4,1)}), s8[4194304]{0:T(1024)(128)(4,1)S(1)}, s32[]{:S(2)}) async-start(s8[4718592]{0:T(1024)(128)(4,1)} %bitcast.12), calls=%async_computation.1 | async-start | bytes 8388608
  77.2 79.5 %slice-start.1 = ((s8[4718592]{0:T(1024)(128)(4,1)}), s8[524288]{0:T(1024)(128)(4,1)S(1)}, s32[]{:S(2)}) async-start(s8[4718592]{0:T(1024)(128)(4,1)} %bitcast.12), calls=%async_computation.2 | async-start | bytes 1048576
  86.1 17.7 %collective-permute-start.17 = (bf16[2,48,2048]{2,1,0:T(8,128)(2,1)S(1)}, bf16[2,48,2048]{2,1,0:T(8,128)(2,1)S(1)}, u32[]{:S(2)}, u32[]{:S(2)}) collective-permute-start(bf16[2,48,2048]{2,1,0:T(8,128)(2,1)S(1)} %get-tuple-element.129), channel_id=1, source_target_pairs={{0,10},{1,11},{2,8},{4,14},{6,12},{7,13},{8,2},{10,0},{11,1},{12,6... | collective-permute-start | bytes 1179656 | tf_op jit(solution)/shard_map/ppermute | solution.py:538
  90.9 14.2 %collective-permute-start.13 = (bf16[2,48,2048]{2,1,0:T(8,128)(2,1)S(1)}, bf16[2,48,2048]{2,1,0:T(8,128)(2,1)S(1)}, u32[]{:S(2)}, u32[]{:S(2)}) collective-permute-start(bf16[2,48,2048]{2,1,0:T(8,128)(2,1)S(1)} %get-tuple-element.118), channel_id=1, source_target_pairs={{0,8},{1,9},{2,10},{4,12},{6,14},{7,15},{8,0},{10,2},{11,3},{12,4}... | collective-permute-start | bytes 1179656 | tf_op jit(solution)/shard_map/ppermute | solution.py:538
  95.2 15.6 %collective-permute-start.14 = (bf16[2,64,2048]{2,1,0:T(8,128)(2,1)S(1)}, bf16[2,64,2048]{2,1,0:T(8,128)(2,1)S(1)}, u32[]{:S(2)}, u32[]{:S(2)}) collective-permute-start(bf16[2,64,2048]{2,1,0:T(8,128)(2,1)S(1)} %get-tuple-element.121), channel_id=1, source_target_pairs={{0,2},{1,3},{2,0},{3,1},{4,6},{6,4},{7,5},{8,10},{9,11},{10,8},{11... | collective-permute-start | bytes 1572872 | tf_op jit(solution)/shard_map/ppermute | solution.py:538
  97.1 13.7 %collective-permute-start.15 = (bf16[2,64,2048]{2,1,0:T(8,128)(2,1)S(1)}, bf16[2,64,2048]{2,1,0:T(8,128)(2,1)S(1)}, u32[]{:S(2)}, u32[]{:S(2)}) collective-permute-start(bf16[2,64,2048]{2,1,0:T(8,128)(2,1)S(1)} %get-tuple-element.122), channel_id=1, source_target_pairs={{0,4},{1,5},{2,6},{3,7},{4,0},{6,2},{7,3},{8,12},{9,13},{10,14},{1... | collective-permute-start | bytes 1572872 | tf_op jit(solution)/shard_map/ppermute | solution.py:538
  98.4 23.5 %collective-permute-start.16 = (bf16[2,64,2048]{2,1,0:T(8,128)(2,1)S(1)}, bf16[2,64,2048]{2,1,0:T(8,128)(2,1)S(1)}, u32[]{:S(2)}, u32[]{:S(2)}) collective-permute-start(bf16[2,64,2048]{2,1,0:T(8,128)(2,1)S(1)} %get-tuple-element.123), channel_id=1, source_target_pairs={{0,6},{1,7},{2,4},{3,5},{4,2},{6,0},{7,1},{8,14},{9,15},{10,12},{1... | collective-permute-start | bytes 1572872 | tf_op jit(solution)/shard_map/ppermute | solution.py:538
  103.8 54.9 %collective-permute-start.19 = (bf16[2,48,2048]{2,1,0:T(8,128)(2,1)S(1)}, bf16[2,48,2048]{2,1,0:T(8,128)(2,1)S(1)}, u32[]{:S(2)}, u32[]{:S(2)}) collective-permute-start(bf16[2,48,2048]{2,1,0:T(8,128)(2,1)S(1)} %get-tuple-element.132), channel_id=1, source_target_pairs={{0,14},{1,15},{2,12},{4,10},{6,8},{7,9},{8,6},{10,4},{11,5},{12,2}... | collective-permute-start | bytes 1179656 | tf_op jit(solution)/shard_map/ppermute | solution.py:538
  105.1 53.6 %collective-permute-start.18 = (bf16[2,48,2048]{2,1,0:T(8,128)(2,1)S(1)}, bf16[2,48,2048]{2,1,0:T(8,128)(2,1)S(1)}, u32[]{:S(2)}, u32[]{:S(2)}) collective-permute-start(bf16[2,48,2048]{2,1,0:T(8,128)(2,1)S(1)} %get-tuple-element.131), channel_id=1, source_target_pairs={{0,12},{1,13},{2,14},{4,8},{6,10},{7,11},{8,4},{10,6},{11,7},{12,0... | collective-permute-start | bytes 1179656 | tf_op jit(solution)/shard_map/ppermute | solution.py:538
  122.6 39.4 %collective-permute-start.23 = (bf16[5,48,2048]{2,1,0:T(8,128)(2,1)S(1)}, bf16[5,48,2048]{2,1,0:T(8,128)(2,1)S(1)}, u32[]{:S(2)}, u32[]{:S(2)}) collective-permute-start(bf16[5,48,2048]{2,1,0:T(8,128)(2,1)S(1)} %get-tuple-element.134), channel_id=1, source_target_pairs={{0,1},{1,0},{2,3},{3,2},{4,5},{5,4},{6,7},{7,6},{8,9},{9,8},{10,11... | collective-permute-start | bytes 2949128 | tf_op jit(solution)/shard_map/ppermute | solution.py:538
  143.8 16.6 %collective-permute-start.21 = (bf16[2,32,2048]{2,1,0:T(8,128)(2,1)S(1)}, bf16[2,32,2048]{2,1,0:T(8,128)(2,1)S(1)}, u32[]{:S(2)}, u32[]{:S(2)}) collective-permute-start(bf16[2,32,2048]{2,1,0:T(8,128)(2,1)S(1)} %get-tuple-element.133), channel_id=1, source_target_pairs={{1,9},{3,11},{5,13},{7,15},{9,1},{11,3},{13,5},{15,7},{17,25},{19,... | collective-permute-start | bytes 786440 | tf_op jit(solution)/shard_map/ppermute | solution.py:538
  159.3 8.3 %collective-permute-start.20 = (bf16[4,48,2048]{2,1,0:T(8,128)(2,1)S(1)}, bf16[4,48,2048]{2,1,0:T(8,128)(2,1)S(1)}, u32[]{:S(2)}, u32[]{:S(2)}) collective-permute-start(bf16[4,48,2048]{2,1,0:T(8,128)(2,1)S(1)} %gather.2), channel_id=1, source_target_pairs={{0,1},{1,0},{2,3},{3,2},{4,5},{5,4},{6,7},{7,6},{8,9},{9,8},{10,11... | collective-permute-start | bytes 2359304 | tf_op jit(solution)/shard_map/ppermute | solution.py:538
  160.4 6.0 %collective-permute-start.22 = (bf16[32,2048]{1,0:T(8,128)(2,1)S(1)}, bf16[32,2048]{1,0:T(8,128)(2,1)S(1)}, u32[]{:S(2)}, u32[]{:S(2)}) collective-permute-start(bf16[32,2048]{1,0:T(8,128)(2,1)S(1)} %slice_bitcast_fusion), channel_id=1, source_target_pairs={{1,0},{3,2},{5,4},{7,6},{9,8},{11,10},{13,12},{15,14},{17,16},{19,... | collective-permute-start | bytes 393224 | tf_op jit(solution)/shard_map/ppermute | solution.py:538
  (11 other events, 68.4 us)

commit v2 on v1

--- a/solution.py
+++ b/solution.py
@@ -107,41 +107,43 @@
     )(eg, em)
 
 
-def stage_kernel(devices, me, held, total, gv, mv, kg, km, partial, staged, keep, away):
+def stage_kernel(devices, me, kinds, held, total, gv, mv, kg, km, partial, staged, away):
     squares = jnp.sum(total[...]) + jnp.sum(fold(kg[...], math.gcd(8, kg.shape[1])))
     partial[...] = jnp.full(partial.shape, squares, F32)
     mine = (me[0] >= devices // 2).astype(jnp.int32)
-    for out, index in ((keep, mine), (away, 1 - mine)):
-        out[0] = kg[index].astype(BF16)
-        out[1] = km[index].astype(BF16)
+    away[0] = kg[1 - mine].astype(BF16)
+    away[1] = km[1 - mine].astype(BF16)
     chips = staged.shape[1]
     for step in range(chips):
         expert = held[me[0] * chips + step]
         staged[0, step] = gv[expert].astype(BF16)
         staged[1, step] = mv[expert].astype(BF16)
 
+        @pl.when(kinds[me[0] * chips + step] == 2)
+        def _():
+            staged[0, step, : kg.shape[1]] = kg[mine].astype(BF16)
+            staged[1, step, : kg.shape[1]] = km[mine].astype(BF16)
+
 
 def stage(me, table, total, gv, mv, kg, km):
     _, rows, width = gv.shape
     devices = table.shape[1]
     chips = devices // 2
-    _, held = visits(table, [2 * step + 1 for step in range(chips)])
+    kinds, held = visits(table, [2 * step + 1 for step in range(chips)])
     vmem = pl.BlockSpec(memory_space=pltpu.VMEM)
     smem = pl.BlockSpec(memory_space=pltpu.SMEM)
-    kv = jax.ShapeDtypeStruct((2,) + kg.shape[1:], BF16)
     return pl.pallas_call(
         functools.partial(stage_kernel, devices),
-        in_specs=[smem] * 2 + [vmem] * 5,
-        out_specs=[vmem] * 4,
+        in_specs=[smem] * 3 + [vmem] * 5,
+        out_specs=[vmem] * 3,
         out_shape=[
             jax.ShapeDtypeStruct((devices, 8, 128), F32),
             jax.ShapeDtypeStruct((2, chips, rows, width), BF16),
-            kv,
-            kv,
+            jax.ShapeDtypeStruct((2,) + kg.shape[1:], BF16),
         ],
         compiler_params=pltpu.CompilerParams(vmem_limit_bytes=STREAM_LIMIT),
         name="stage",
-    )(me, held, total, gv, mv, kg, km)
+    )(me, kinds, held, total, gv, mv, kg, km)
 
 
 def nesterov(scale, grad, moment):
@@ -152,8 +154,8 @@
 def form_far_kernel(count, start, me, kinds, index, squares, gv, mv, sib, clip, *outs):
     total = jnp.sum(squares[...], axis=0)
     factor = jnp.minimum(1.0, count / (jnp.sqrt(total) + CLIP_EPS))
-    clip[...] = factor
     scale = factor[0:1, 0:1]
+    clip[...] = scale
     for step, out in enumerate(outs):
         place = me[0] * len(outs) + step
 
@@ -163,8 +165,8 @@
             out[1] = nesterov(scale, sib[0, start + step], sib[1, start + step])
 
 
-def form_near_kernel(me, kinds, index, clip, gv, mv, sib, kg, km, mirror, kv_sib, *outs):
-    scale = clip[0:1, 0:1]
+def form_near_kernel(me, kinds, index, clip, gv, mv, sib, kg, km, mirror, mirror_sib, *outs):
+    scale = clip[...]
     steps, kv_rows = len(outs) // 2, kg.shape[1]
     mine = (me[0] >= kinds.shape[0] // steps // 2).astype(jnp.int32)
     for step, (out, kv) in enumerate(zip(outs[:steps], outs[steps:])):
@@ -179,8 +181,8 @@
         def _():
             kv[0, :kv_rows] = nesterov(scale, kg[mine], km[mine])
             kv[0, kv_rows:] = nesterov(scale, mirror[0], mirror[1])
-            kv[1, :kv_rows] = nesterov(scale, kv_sib[0, 0], kv_sib[0, 1])
-            kv[1, kv_rows:] = nesterov(scale, kv_sib[1, 0], kv_sib[1, 1])
+            kv[1, :kv_rows] = nesterov(scale, sib[0, step, :kv_rows], sib[1, step, :kv_rows])
+            kv[1, kv_rows:] = nesterov(scale, mirror_sib[0], mirror_sib[1])
 
 
 def form_call(kernel, name, table, chip_steps, me, operands, outs):
@@ -199,18 +201,18 @@
 
 def form_far(me, table, steps, squares, gv, mv, sib, count):
     block = jax.ShapeDtypeStruct((2,) + gv.shape[1:], BF16)
-    clip = jax.ShapeDtypeStruct((8, 128), F32)
+    clip = jax.ShapeDtypeStruct((1, 1), F32)
     kernel = functools.partial(form_far_kernel, count, steps[0])
     return form_call(
         kernel, "far", table, steps, me, (squares, gv, mv, sib), [clip] + [block] * len(steps)
     )
 
 
-def form_near(me, table, steps, clip, gv, mv, sib, kg, km, mirror, kv_sib):
+def form_near(me, table, steps, clip, gv, mv, sib, kg, km, mirror, mirror_sib):
     _, rows, width = gv.shape
     shapes = [(2, rows, width)] * len(steps) + [(2, 2 * kg.shape[1], width)] * len(steps)
     outs = [jax.ShapeDtypeStruct(shape, BF16) for shape in shapes]
-    operands = (clip, gv, mv, sib, kg, km, mirror, kv_sib)
+    operands = (clip, gv, mv, sib, kg, km, mirror, mirror_sib)
     blocks = form_call(form_near_kernel, "form", table, steps, me, operands, outs)
     return list(blocks[: len(steps)]), list(blocks[len(steps) :])
 
@@ -574,20 +576,23 @@
     near_steps, far_steps = list(range(half)), list(range(half, chips))
 
     total, gv, mv = load(eg, em)
-    partial, staged, keep, away = stage(me, table, total, gv, mv, kv_grad, kv_momentum)
-    mirror = permute(away, mirrors)
+    partial, staged, away = stage(me, table, total, gv, mv, kv_grad, kv_momentum)
+    mirror = permute(away, [pair for pair in mirrors if pair[0] % 2])
+    mirror_sib = permute(away, [(here, there ^ 1) for here, there in mirrors if here % 2 == 0])
     squares = lax.all_to_all(partial, "fsdp", 0, 0, tiled=True)
-    squares, sibling, mirror = together(squares, permute(staged, cores), mirror)
+    squares, sibling, mirror, mirror_sib = together(
+        squares, permute(staged, cores), mirror, mirror_sib
+    )
 
     clip, *far = form_far(me, table, far_steps, squares, gv, mv, sibling, count)
-    clip, far[0], keep = together(clip, far[0], keep)
-    kv_sibling = permute(jnp.stack([keep, mirror]), [pair for pair in cores if pair[1] % 2])
+    clip, far[0] = together(clip, far[0])
     near, kv = form_near(
-        me, table, near_steps, clip, gv, mv, sibling, kv_grad, kv_momentum, mirror, kv_sibling
+        me, table, near_steps, clip, gv, mv, sibling, kv_grad, kv_momentum, mirror, mirror_sib
     )
     far = cross(far, table, far_steps, True)
     for step in near_steps[1:]:
         near[step] = permute(near[step], block_pairs(table, step, True))
+        kv[step], near[step] = together(kv[step], near[step])
         kv[step] = permute(kv[step], block_pairs(table, step, True, (2,)))
     kinds = jnp.asarray(table[0])
 

time: 171 us -> 177 us (1.035)
  waiting for transfers between devices: 30.8 us -> 73.2 us
  starting transfers between devices: 84.6 us -> 48.4 us
  Pallas kernels: 32.6 us -> 34.6 us
    ppermute x24, waiting for transfers between devices: 30.8 us -> 73.2 us  [permute(): return lax.ppermute(array, 'fsdp', pairs)]
    ppermute x24, starting transfers between devices: 84.6 us -> 48.4 us  [permute(): return lax.ppermute(array, 'fsdp', pairs)]
    pallas_call x2, Pallas kernels: 2.77 us -> 4.71 us  [form_call(): pl.pallas_call(kernel, in_specs=[smem] * 3 + [vmem] * len(operands), out_...]
  transfers between devices with their start and end apart: 24 -> 24, of which waited for: 7 -> 9; matrix products, arithmetic and copies ran while one was open for 4% -> 3% of each run, Pallas kernels for 9% -> 9%
where the time goes in v2:
time: 177 us
  waiting for transfers between devices  73.2 us (41%)
  starting transfers between devices  48.4 us (27%)
  Pallas kernels  34.6 us (20%)
  blocking collectives  13.3 us (8%)
  other arithmetic  5.84 us (3%)
    ppermute x24, waiting for transfers between devices, permute(): return lax.ppermute(array, 'fsdp', pairs)  73.2 us
    ppermute x24, starting transfers between devices, permute(): return lax.ppermute(array, 'fsdp', pairs)  48.4 us
    all_to_all x1, blocking collectives, shards(): squares = lax.all_to_all(partial, 'fsdp', 0, 0, tiled=True)  13.3 us
    pallas_call x3, Pallas kernels, finish(): pl.pallas_call(functools.partial(finish_kernel, (own, sibling is not None...  9.24 us
    pallas_call x1, Pallas kernels, orthogonal_update(): pl.pallas_call(functools.partial(transform_kernel, gain, kv_rows), in_spe...  8.92 us
    pallas_call x2, Pallas kernels, form_call(): pl.pallas_call(kernel, in_specs=[smem] * 3 + [vmem] * len(operands), out_...  4.71 us
    add x1, other arithmetic, shards(): expert_moment_out = MOMENTUM * expert_momentum + factor * expert_grad  4.34 us
    pallas_call x1, Pallas kernels, load(): pl.pallas_call(load_kernel, in_specs=[hbm] * 2, out_specs=[vmem] * 3, out...  3.86 us
  transfers between devices with their start and end apart: 24, of which 9 were waited for; matrix products, arithmetic and copies ran while one was open for 3% of the time, Pallas kernels for 9%

profile of v2, /device:TPU:1, one launch (start us, length us, event | category | flops | bytes accessed | tf_op | source)
XLA Modules:
  0.0 176.8 jit_solution(17045355969179397736)
XLA Ops:
  0.7 3.9 %load.1 = (f32[8,2048]{1,0:T(8,128)S(1)}, f32[12,48,2048]{2,1,0:T(8,128)S(1)}, f32[12,48,2048]{2,1,0:T(8,128)S(1)}) custom-call(f32[12,48,2048]{2,1,0:T(8,128)} %bitcast.16, f32[12,48,2048]{2,1,0:T(8,128)} %bitcast.19), custom_call_target="tpu_custom_call" | custom-call | tf_op jit(solution)/shard_map/load/pallas_call | solution.py:99
  5.9 5.6 %collective-permute-start.1 = (bf16[2,32,2048]{2,1,0:T(8,128)(2,1)S(1)}, bf16[2,32,2048]{2,1,0:T(8,128)(2,1)S(1)}, u32[]{:S(2)}, u32[]{:S(2)}) collective-permute-start(bf16[2,32,2048]{2,1,0:T(8,128)(2,1)S(1)} %get-tuple-element.91), channel_id=1, source_target_pairs={{1,9},{3,11},{5,13},{7,15},{9,1},{11,3},{13,5},{15,7},{17,25},{19,... | collective-permute-start | bytes 786440 | tf_op jit(solution)/shard_map/ppermute | solution.py:540
  12.8 13.3 %all_to_all.5.squares = f32[16,8,128]{2,1,0:T(8,128)S(1)} all-to-all(f32[16,8,128]{2,1,0:T(8,128)S(1)} %get-tuple-element.89), channel_id=1, replica_groups=mesh['groups'=2,'fsdp'=16] {'fsdp'}, dimensions={0} | all-to-all | bytes 131072 | tf_op jit(solution)/shard_map/all_to_all | solution.py:582
  26.2 1.7 far.1
  27.9 4.1 %collective-permute-start.10 = (bf16[2,48,2048]{2,1,0:T(8,128)(2,1)S(1)}, bf16[2,48,2048]{2,1,0:T(8,128)(2,1)S(1)}, u32[]{:S(2)}, u32[]{:S(2)}) collective-permute-start(bf16[2,48,2048]{2,1,0:T(8,128)(2,1)S(1)} %get-tuple-element.120), channel_id=1, source_target_pairs={{10,0},{11,1},{8,2},{14,4},{12,6},{13,7},{2,8},{0,10},{1,11},{6,12... | collective-permute-start | bytes 1179656 | tf_op jit(solution)/shard_map/ppermute | solution.py:540
  32.1 1.6 collective-permute-start.9
  33.6 3.0 %form.1 = (bf16[2,48,2048]{2,1,0:T(8,128)(2,1)S(1)}, bf16[2,48,2048]{2,1,0:T(8,128)(2,1)S(1)}, bf16[2,48,2048]{2,1,0:T(8,128)(2,1)S(1)}, bf16[2,48,2048]{2,1,0:T...) custom-call(s32[1]{0:T(128)} %bitcast.me, ...), custom_call_target="tpu_custom_call" | custom-call | tf_op jit(solution)/shard_map/form/pallas_call | solution.py:192
  36.7 4.1 %collective-permute-start.5 = (bf16[2,48,2048]{2,1,0:T(8,128)(2,1)S(1)}, bf16[2,48,2048]{2,1,0:T(8,128)(2,1)S(1)}, u32[]{:S(2)}, u32[]{:S(2)}) collective-permute-start(bf16[2,48,2048]{2,1,0:T(8,128)(2,1)S(1)} %get-tuple-element.108), channel_id=1, source_target_pairs={{6,0},{7,1},{4,2},{2,4},{0,6},{1,7},{14,8},{12,10},{13,11},{10,12}... | collective-permute-start | bytes 1179656 | tf_op jit(solution)/shard_map/ppermute | solution.py:540
  43.4 4.3 %multiply_add_fusion = f32[4,3,48,2048]{3,2,1,0:T(8,128)} fusion(f32[4,3,48,2048]{3,2,1,0:T(8,128)S(1)} %bitcast.18, f32[4,3,48,2048]{3,2,1,0:T(8,128)S(1)} %bitcast.21, f32[]{:T(128)} %bitcast.3), kind=kLoop, calls=%fused_computation | loop fusion | flops 3538944 | bytes 14155780 | tf_op jit(solution)/shard_map/add | solution.py:600
  47.7 6.1 %collective-permute-done.10.refs_5_ = bf16[2,48,2048]{2,1,0:T(8,128)(2,1)S(1)} collective-permute-done((bf16[2,48,2048]{2,1,0:T(8,128)(2,1)S(1)}, bf16[2,48,2048]{2,1,0:T(8,128)(2,1)S(1)}, u32[]{:S(2)}, u32[]{:S(2)}) %collective-permute-start.10) | collective-permute-done | bytes 393248 | tf_op jit(solution)/shard_map/ppermute | solution.py:540
  55.4 4.9 %collective-permute-start.11 = (bf16[2,48,2048]{2,1,0:T(8,128)(2,1)S(1)}, bf16[2,48,2048]{2,1,0:T(8,128)(2,1)S(1)}, u32[]{:S(2)}, u32[]{:S(2)}) collective-permute-start(bf16[2,48,2048]{2,1,0:T(8,128)(2,1)S(1)} %get-tuple-element.122), channel_id=1, source_target_pairs={{12,0},{13,1},{14,2},{8,4},{10,6},{11,7},{4,8},{6,10},{7,11},{0,12... | collective-permute-start | bytes 1179656 | tf_op jit(solution)/shard_map/ppermute | solution.py:540
  60.3 12.9 %collective-permute-done.4.refs_2_ = bf16[2,48,2048]{2,1,0:T(8,128)(2,1)S(1)} collective-permute-done((bf16[2,48,2048]{2,1,0:T(8,128)(2,1)S(1)}, bf16[2,48,2048]{2,1,0:T(8,128)(2,1)S(1)}, u32[]{:S(2)}, u32[]{:S(2)}) %collective-permute-start.4) | collective-permute-done | bytes 393248 | tf_op jit(solution)/shard_map/ppermute | solution.py:540
  75.6 2.4 %collective-permute-start.6 = (bf16[2,64,2048]{2,1,0:T(8,128)(2,1)S(1)}, bf16[2,64,2048]{2,1,0:T(8,128)(2,1)S(1)}, u32[]{:S(2)}, u32[]{:S(2)}) collective-permute-start(bf16[2,64,2048]{2,1,0:T(8,128)(2,1)S(1)} %get-tuple-element.113), channel_id=1, source_target_pairs={{1,3},{11,9},{17,19},{27,25}} | collective-permute-start | bytes 1572872 | tf_op jit(solution)/shard_map/ppermute | solution.py:540
  78.0 1.5 multiply_add_fusion.1
  79.5 1.5 near.1
  81.1 7.8 %collective-permute-done.6.refs_1_ = bf16[2,64,2048]{2,1,0:T(8,128)(2,1)S(1)} collective-permute-done((bf16[2,64,2048]{2,1,0:T(8,128)(2,1)S(1)}, bf16[2,64,2048]{2,1,0:T(8,128)(2,1)S(1)}, u32[]{:S(2)}, u32[]{:S(2)}) %collective-permute-start.6) | collective-permute-done | bytes 524320 | tf_op jit(solution)/shard_map/ppermute | solution.py:540
  88.9 8.9 %transform.1 = (bf16[768,2048]{1,0:T(8,128)(2,1)S(1)}, bf16[768,768]{1,0:T(8,128)(2,1)S(1)}, f32[768,128]{1,0:T(8,128)S(1)}, bf16[2,48,2048]{2,1,0:T(8,128)(2,1)S(1)}, bf16[2,48,2048]{2,1,0:T(8,128)(2,1)S(1)}) custom-call(s32[1]{0:T(128)} %bitcast.me, s32[16]{0:T(128)S(1)} %copy-done.5, bf16[384,2048]{1,0:T(8,128)(2,1)S(1)} %get-tuple-element.110.near, ...), custom_call_target="tpu_custom_call" | custom-call | tf_op jit(solution)/shard_map/transform/pallas_call | solution.py:367
  97.8 1.9 %collective-permute-start.17 = (bf16[2,48,2048]{2,1,0:T(8,128)(2,1)S(1)}, bf16[2,48,2048]{2,1,0:T(8,128)(2,1)S(1)}, u32[]{:S(2)}, u32[]{:S(2)}) collective-permute-start(bf16[2,48,2048]{2,1,0:T(8,128)(2,1)S(1)} %get-tuple-element.139), channel_id=1, source_target_pairs={{0,10},{1,11},{2,8},{4,14},{6,12},{7,13},{8,2},{10,0},{11,1},{12,6... | collective-permute-start | bytes 1179656 | tf_op jit(solution)/shard_map/ppermute | solution.py:540
  101.1 2.9 %apply.1 = (bf16[2,64,2048]{2,1,0:T(8,128)(2,1)S(1)}, bf16[2,64,2048]{2,1,0:T(8,128)(2,1)S(1)}, bf16[2,64,2048]{2,1,0:T(8,128)(2,1)S(1)}, bf16[2,64,2048]{2,1,0:...) custom-call(s32[1]{0:T(128)} %bitcast.me, s32[16]{0:T(128)S(1)} %copy-done.5, ...), custom_call_target="tpu_custom_call" | custom-call | tf_op jit(solution)/shard_map/apply/pallas_call | solution.py:382
  104.0 1.9 %collective-permute-start.14 = (bf16[2,64,2048]{2,1,0:T(8,128)(2,1)S(1)}, bf16[2,64,2048]{2,1,0:T(8,128)(2,1)S(1)}, u32[]{:S(2)}, u32[]{:S(2)}) collective-permute-start(bf16[2,64,2048]{2,1,0:T(8,128)(2,1)S(1)} %get-tuple-element.131), channel_id=1, source_target_pairs={{0,2},{1,3},{2,0},{3,1},{4,6},{6,4},{7,5},{8,10},{9,11},{10,8},{11... | collective-permute-start | bytes 1572872 | tf_op jit(solution)/shard_map/ppermute | solution.py:540
  106.0 1.3 collective-permute-start.15
  107.3 5.1 %collective-permute-start.16 = (bf16[2,64,2048]{2,1,0:T(8,128)(2,1)S(1)}, bf16[2,64,2048]{2,1,0:T(8,128)(2,1)S(1)}, u32[]{:S(2)}, u32[]{:S(2)}) collective-permute-start(bf16[2,64,2048]{2,1,0:T(8,128)(2,1)S(1)} %get-tuple-element.133), channel_id=1, source_target_pairs={{0,6},{1,7},{2,4},{3,5},{4,2},{6,0},{7,1},{8,14},{9,15},{10,12},{1... | collective-permute-start | bytes 1572872 | tf_op jit(solution)/shard_map/ppermute | solution.py:540
  112.4 5.4 %collective-permute-done.17.refs_1_ = bf16[2,48,2048]{2,1,0:T(8,128)(2,1)S(1)} collective-permute-done((bf16[2,48,2048]{2,1,0:T(8,128)(2,1)S(1)}, bf16[2,48,2048]{2,1,0:T(8,128)(2,1)S(1)}, u32[]{:S(2)}, u32[]{:S(2)}) %collective-permute-start.17) | collective-permute-done | bytes 393248 | tf_op jit(solution)/shard_map/ppermute | solution.py:540
  119.2 2.2 %collective-permute-start.18 = (bf16[2,48,2048]{2,1,0:T(8,128)(2,1)S(1)}, bf16[2,48,2048]{2,1,0:T(8,128)(2,1)S(1)}, u32[]{:S(2)}, u32[]{:S(2)}) collective-permute-start(bf16[2,48,2048]{2,1,0:T(8,128)(2,1)S(1)} %get-tuple-element.141), channel_id=1, source_target_pairs={{0,12},{1,13},{2,14},{4,8},{6,10},{7,11},{8,4},{10,6},{11,7},{12,0... | collective-permute-start | bytes 1179656 | tf_op jit(solution)/shard_map/ppermute | solution.py:540
  121.4 10.1 %collective-permute-done.14.refs_1_ = bf16[2,64,2048]{2,1,0:T(8,128)(2,1)S(1)} collective-permute-done((bf16[2,64,2048]{2,1,0:T(8,128)(2,1)S(1)}, bf16[2,64,2048]{2,1,0:T(8,128)(2,1)S(1)}, u32[]{:S(2)}, u32[]{:S(2)}) %collective-permute-start.14) | collective-permute-done | bytes 524320 | tf_op jit(solution)/shard_map/ppermute | solution.py:540
  131.4 25.7 %collective-permute-done.16.refs_3_ = bf16[2,64,2048]{2,1,0:T(8,128)(2,1)S(1)} collective-permute-done((bf16[2,64,2048]{2,1,0:T(8,128)(2,1)S(1)}, bf16[2,64,2048]{2,1,0:T(8,128)(2,1)S(1)}, u32[]{:S(2)}, u32[]{:S(2)}) %collective-permute-start.16) | collective-permute-done | bytes 524320 | tf_op jit(solution)/shard_map/ppermute | solution.py:540
  158.3 1.9 %collective-permute-start.21 = (bf16[2,32,2048]{2,1,0:T(8,128)(2,1)S(1)}, bf16[2,32,2048]{2,1,0:T(8,128)(2,1)S(1)}, u32[]{:S(2)}, u32[]{:S(2)}) collective-permute-start(bf16[2,32,2048]{2,1,0:T(8,128)(2,1)S(1)} %get-tuple-element.143), channel_id=1, source_target_pairs={{1,9},{3,11},{5,13},{7,15},{9,1},{11,3},{13,5},{15,7},{17,25},{19,... | collective-permute-start | bytes 786440 | tf_op jit(solution)/shard_map/ppermute | solution.py:540
  160.2 2.0 %finish.3 = (f32[12,48,2048]{2,1,0:T(8,128)}, bf16[12,48,2048]{2,1,0:T(8,128)(2,1)}, bf16[12,48,2048]{2,1,0:T(8,128)(2,1)}) custom-call(s32[1]{0:T(128)} %bitcast.me, s32[64]{0:T(128)S(1)} %copy-done.3, s32[64]{0:T(128)S(1)} %copy-done.4, bf16[2,64,2048]{2,1,0:T(8,128)(2,1)S(1)} %get-tuple-element.130.refs_0_, ...), custom_call_target="tpu_custom_call" | custom-call | tf_op jit(solution)/shard_map/finish/pallas_call | solution.py:522
  162.9 4.0 %collective-permute-done.21.across = bf16[2,32,2048]{2,1,0:T(8,128)(2,1)S(1)} collective-permute-done((bf16[2,32,2048]{2,1,0:T(8,128)(2,1)S(1)}, bf16[2,32,2048]{2,1,0:T(8,128)(2,1)S(1)}, u32[]{:S(2)}, u32[]{:S(2)}) %collective-permute-start.21) | collective-permute-done | bytes 262176 | tf_op jit(solution)/shard_map/ppermute | solution.py:540
  167.0 1.4 collective-permute-start.22
  168.4 4.5 %finish.4 = (f32[12,48,2048]{2,1,0:T(8,128)}, bf16[12,48,2048]{2,1,0:T(8,128)(2,1)}, bf16[12,48,2048]{2,1,0:T(8,128)(2,1)}) custom-call(s32[1]{0:T(128)} %bitcast.me, s32[128]{0:T(128)S(1)} %copy-done.9, s32[128]{0:T(128)S(1)} %copy-done.10, ...), custom_call_target="tpu_custom_call", output_to_operand_aliasing={{0}: (9, {}), {1}: (10, {}), {2}: (11, {})} | custom-call | tf_op jit(solution)/shard_map/finish/pallas_call | solution.py:522
  174.0 2.8 %finish.5 = (f32[12,48,2048]{2,1,0:T(8,128)}, bf16[12,48,2048]{2,1,0:T(8,128)(2,1)}, bf16[12,48,2048]{2,1,0:T(8,128)(2,1)}) custom-call(s32[1]{0:T(128)} %bitcast.me, s32[64]{0:T(128)S(1)} %copy-done.7, s32[64]{0:T(128)S(1)} %copy-done.8, ...), custom_call_target="tpu_custom_call", output_to_operand_aliasing={{0}: (5, {}), {1}: (6, {}), {2}: (7, {})} | custom-call | tf_op jit(solution)/shard_map/finish/pallas_call | solution.py:522
  (76 shorter events, 14.8 us)
Async XLA Ops:
  4.6 21.6 %copy-start.6 = (s32[64]{0:T(128)S(1)}, s32[64]{0:T(128)}, u32[]{:S(2)}) copy-start(s32[64]{0:T(128)} %constant.31.clone.kinds) | copy-start | bytes 772
  4.6 21.6 %copy-start.11 = (s32[64]{0:T(128)S(1)}, s32[64]{0:T(128)}, u32[]{:S(2)}) copy-start(s32[64]{0:T(128)} %constant.32.clone.index) | copy-start | bytes 772
  5.7 20.5 %collective-permute-start = (bf16[2,8,48,2048]{3,2,1,0:T(8,128)(2,1)S(1)}, bf16[2,8,48,2048]{3,2,1,0:T(8,128)(2,1)S(1)}, u32[]{:S(2)}, u32[]{:S(2)}) collective-permute-start(bf16[2,8,48,2048]{3,2,1,0:T(8,128)(2,1)S(1)} %get-tuple-element.90), channel_id=1, source_target_pairs={{0,1},{1,0},{2,3},{3,2},{4,5},{5,4},{6,7},{7,6},{8,9},{9,8},{10,11... | collective-permute-start | bytes 9437192 | tf_op jit(solution)/shard_map/ppermute | solution.py:540
  5.9 20.3 %collective-permute-start.1 = (bf16[2,32,2048]{2,1,0:T(8,128)(2,1)S(1)}, bf16[2,32,2048]{2,1,0:T(8,128)(2,1)S(1)}, u32[]{:S(2)}, u32[]{:S(2)}) collective-permute-start(bf16[2,32,2048]{2,1,0:T(8,128)(2,1)S(1)} %get-tuple-element.91), channel_id=1, source_target_pairs={{1,9},{3,11},{5,13},{7,15},{9,1},{11,3},{13,5},{15,7},{17,25},{19,... | collective-permute-start | bytes 786440 | tf_op jit(solution)/shard_map/ppermute | solution.py:540
  11.5 14.7 %collective-permute-start.2 = (bf16[2,32,2048]{2,1,0:T(8,128)(2,1)S(1)}, bf16[2,32,2048]{2,1,0:T(8,128)(2,1)S(1)}, u32[]{:S(2)}, u32[]{:S(2)}) collective-permute-start(bf16[2,32,2048]{2,1,0:T(8,128)(2,1)S(1)} %get-tuple-element.91), channel_id=1, source_target_pairs={{0,9},{2,11},{4,13},{6,15},{8,1},{10,3},{12,5},{14,7},{16,25},{18,... | collective-permute-start | bytes 786440 | tf_op jit(solution)/shard_map/ppermute | solution.py:540
  27.9 25.9 %collective-permute-start.10 = (bf16[2,48,2048]{2,1,0:T(8,128)(2,1)S(1)}, bf16[2,48,2048]{2,1,0:T(8,128)(2,1)S(1)}, u32[]{:S(2)}, u32[]{:S(2)}) collective-permute-start(bf16[2,48,2048]{2,1,0:T(8,128)(2,1)S(1)} %get-tuple-element.120), channel_id=1, source_target_pairs={{10,0},{11,1},{8,2},{14,4},{12,6},{13,7},{2,8},{0,10},{1,11},{6,12... | collective-permute-start | bytes 1179656 | tf_op jit(solution)/shard_map/ppermute | solution.py:540
  32.0 11.3 %slice-start.2 = ((s8[4718592]{0:T(1024)(128)(4,1)}), s8[4194304]{0:T(1024)(128)(4,1)S(1)}, s32[]{:S(2)}) async-start(s8[4718592]{0:T(1024)(128)(4,1)} %bitcast.17), calls=%async_computation.3 | async-start | bytes 8388608
  32.0 11.3 %slice-start.4 = ((s8[4718592]{0:T(1024)(128)(4,1)}), s8[4194304]{0:T(1024)(128)(4,1)S(1)}, s32[]{:S(2)}) async-start(s8[4718592]{0:T(1024)(128)(4,1)} %bitcast.20), calls=%async_computation.5 | async-start | bytes 8388608
  32.0 11.3 %slice-start.3 = ((s8[4718592]{0:T(1024)(128)(4,1)}), s8[524288]{0:T(1024)(128)(4,1)S(1)}, s32[]{:S(2)}) async-start(s8[4718592]{0:T(1024)(128)(4,1)} %bitcast.17), calls=%async_computation.4 | async-start | bytes 1048576
  32.1 23.4 %collective-permute-start.9 = (bf16[2,48,2048]{2,1,0:T(8,128)(2,1)S(1)}, bf16[2,48,2048]{2,1,0:T(8,128)(2,1)S(1)}, u32[]{:S(2)}, u32[]{:S(2)}) collective-permute-start(bf16[2,48,2048]{2,1,0:T(8,128)(2,1)S(1)} %get-tuple-element.117), channel_id=1, source_target_pairs={{8,0},{9,1},{10,2},{12,4},{14,6},{15,7},{0,8},{2,10},{3,11},{4,12}... | collective-permute-start | bytes 1179656 | tf_op jit(solution)/shard_map/ppermute | solution.py:540
  36.7 23.6 %collective-permute-start.5 = (bf16[2,48,2048]{2,1,0:T(8,128)(2,1)S(1)}, bf16[2,48,2048]{2,1,0:T(8,128)(2,1)S(1)}, u32[]{:S(2)}, u32[]{:S(2)}) collective-permute-start(bf16[2,48,2048]{2,1,0:T(8,128)(2,1)S(1)} %get-tuple-element.108), channel_id=1, source_target_pairs={{6,0},{7,1},{4,2},{2,4},{0,6},{1,7},{14,8},{12,10},{13,11},{10,12}... | collective-permute-start | bytes 1179656 | tf_op jit(solution)/shard_map/ppermute | solution.py:540
  40.7 32.4 %collective-permute-start.4 = (bf16[2,48,2048]{2,1,0:T(8,128)(2,1)S(1)}, bf16[2,48,2048]{2,1,0:T(8,128)(2,1)S(1)}, u32[]{:S(2)}, u32[]{:S(2)}) collective-permute-start(bf16[2,48,2048]{2,1,0:T(8,128)(2,1)S(1)} %get-tuple-element.105), channel_id=1, source_target_pairs={{4,0},{5,1},{6,2},{0,4},{2,6},{3,7},{12,8},{14,10},{15,11},{8,12},... | collective-permute-start | bytes 1179656 | tf_op jit(solution)/shard_map/ppermute | solution.py:540
  42.0 32.2 %collective-permute-start.3 = (bf16[2,48,2048]{2,1,0:T(8,128)(2,1)S(1)}, bf16[2,48,2048]{2,1,0:T(8,128)(2,1)S(1)}, u32[]{:S(2)}, u32[]{:S(2)}) collective-permute-start(bf16[2,48,2048]{2,1,0:T(8,128)(2,1)S(1)} %get-tuple-element.102), channel_id=1, source_target_pairs={{2,0},{3,1},{0,2},{6,4},{4,6},{5,7},{10,8},{8,10},{9,11},{14,12},{... | collective-permute-start | bytes 1179656 | tf_op jit(solution)/shard_map/ppermute | solution.py:540
  43.4 36.1 %copy-start.5 = (s32[16]{0:T(128)S(1)}, s32[16]{0:T(128)}, u32[]{:S(2)}) copy-start(s32[16]{0:T(128)} %constant.35.clone.kinds) | copy-start | bytes 196
  53.9 27.2 %collective-permute-start.12 = (bf16[2,48,2048]{2,1,0:T(8,128)(2,1)S(1)}, bf16[2,48,2048]{2,1,0:T(8,128)(2,1)S(1)}, u32[]{:S(2)}, u32[]{:S(2)}) collective-permute-start(bf16[2,48,2048]{2,1,0:T(8,128)(2,1)S(1)} %get-tuple-element.123), channel_id=1, source_target_pairs={{14,0},{15,1},{12,2},{10,4},{8,6},{9,7},{6,8},{4,10},{5,11},{2,12}... | collective-permute-start | bytes 1179656 | tf_op jit(solution)/shard_map/ppermute | solution.py:540
  55.4 25.6 %collective-permute-start.11 = (bf16[2,48,2048]{2,1,0:T(8,128)(2,1)S(1)}, bf16[2,48,2048]{2,1,0:T(8,128)(2,1)S(1)}, u32[]{:S(2)}, u32[]{:S(2)}) collective-permute-start(bf16[2,48,2048]{2,1,0:T(8,128)(2,1)S(1)} %get-tuple-element.122), channel_id=1, source_target_pairs={{12,0},{13,1},{14,2},{8,4},{10,6},{11,7},{4,8},{6,10},{7,11},{0,12... | collective-permute-start | bytes 1179656 | tf_op jit(solution)/shard_map/ppermute | solution.py:540
  74.2 6.9 %collective-permute-start.8 = (bf16[2,64,2048]{2,1,0:T(8,128)(2,1)S(1)}, bf16[2,64,2048]{2,1,0:T(8,128)(2,1)S(1)}, u32[]{:S(2)}, u32[]{:S(2)}) collective-permute-start(bf16[2,64,2048]{2,1,0:T(8,128)(2,1)S(1)} %get-tuple-element.115), channel_id=1, source_target_pairs={{5,3},{15,9},{21,19},{31,25}} | collective-permute-start | bytes 1572872 | tf_op jit(solution)/shard_map/ppermute | solution.py:540
  74.9 6.2 %collective-permute-start.7 = (bf16[2,64,2048]{2,1,0:T(8,128)(2,1)S(1)}, bf16[2,64,2048]{2,1,0:T(8,128)(2,1)S(1)}, u32[]{:S(2)}, u32[]{:S(2)}) collective-permute-start(bf16[2,64,2048]{2,1,0:T(8,128)(2,1)S(1)} %get-tuple-element.114), channel_id=1, source_target_pairs={{7,3},{13,9},{23,19},{29,25}} | collective-permute-start | bytes 1572872 | tf_op jit(solution)/shard_map/ppermute | solution.py:540
  75.6 13.3 %collective-permute-start.6 = (bf16[2,64,2048]{2,1,0:T(8,128)(2,1)S(1)}, bf16[2,64,2048]{2,1,0:T(8,128)(2,1)S(1)}, u32[]{:S(2)}, u32[]{:S(2)}) collective-permute-start(bf16[2,64,2048]{2,1,0:T(8,128)(2,1)S(1)} %get-tuple-element.113), channel_id=1, source_target_pairs={{1,3},{11,9},{17,19},{27,25}} | collective-permute-start | bytes 1572872 | tf_op jit(solution)/shard_map/ppermute | solution.py:540
  79.5 80.7 %slice-start = ((s8[4718592]{0:T(1024)(128)(4,1)}), s8[4194304]{0:T(1024)(128)(4,1)S(1)}, s32[]{:S(2)}) async-start(s8[4718592]{0:T(1024)(128)(4,1)} %bitcast.10), calls=%async_computation.1 | async-start | bytes 8388608
  88.9 71.3 %slice-start.1 = ((s8[4718592]{0:T(1024)(128)(4,1)}), s8[524288]{0:T(1024)(128)(4,1)S(1)}, s32[]{:S(2)}) async-start(s8[4718592]{0:T(1024)(128)(4,1)} %bitcast.10), calls=%async_computation.2 | async-start | bytes 1048576
  97.8 20.0 %collective-permute-start.17 = (bf16[2,48,2048]{2,1,0:T(8,128)(2,1)S(1)}, bf16[2,48,2048]{2,1,0:T(8,128)(2,1)S(1)}, u32[]{:S(2)}, u32[]{:S(2)}) collective-permute-start(bf16[2,48,2048]{2,1,0:T(8,128)(2,1)S(1)} %get-tuple-element.139), channel_id=1, source_target_pairs={{0,10},{1,11},{2,8},{4,14},{6,12},{7,13},{8,2},{10,0},{11,1},{12,6... | collective-permute-start | bytes 1179656 | tf_op jit(solution)/shard_map/ppermute | solution.py:540
  99.8 19.4 %collective-permute-start.13 = (bf16[2,48,2048]{2,1,0:T(8,128)(2,1)S(1)}, bf16[2,48,2048]{2,1,0:T(8,128)(2,1)S(1)}, u32[]{:S(2)}, u32[]{:S(2)}) collective-permute-start(bf16[2,48,2048]{2,1,0:T(8,128)(2,1)S(1)} %get-tuple-element.128), channel_id=1, source_target_pairs={{0,8},{1,9},{2,10},{4,12},{6,14},{7,15},{8,0},{10,2},{11,3},{12,4}... | collective-permute-start | bytes 1179656 | tf_op jit(solution)/shard_map/ppermute | solution.py:540
  104.0 27.4 %collective-permute-start.14 = (bf16[2,64,2048]{2,1,0:T(8,128)(2,1)S(1)}, bf16[2,64,2048]{2,1,0:T(8,128)(2,1)S(1)}, u32[]{:S(2)}, u32[]{:S(2)}) collective-permute-start(bf16[2,64,2048]{2,1,0:T(8,128)(2,1)S(1)} %get-tuple-element.131), channel_id=1, source_target_pairs={{0,2},{1,3},{2,0},{3,1},{4,6},{6,4},{7,5},{8,10},{9,11},{10,8},{11... | collective-permute-start | bytes 1572872 | tf_op jit(solution)/shard_map/ppermute | solution.py:540
  106.0 25.5 %collective-permute-start.15 = (bf16[2,64,2048]{2,1,0:T(8,128)(2,1)S(1)}, bf16[2,64,2048]{2,1,0:T(8,128)(2,1)S(1)}, u32[]{:S(2)}, u32[]{:S(2)}) collective-permute-start(bf16[2,64,2048]{2,1,0:T(8,128)(2,1)S(1)} %get-tuple-element.132), channel_id=1, source_target_pairs={{0,4},{1,5},{2,6},{3,7},{4,0},{6,2},{7,3},{8,12},{9,13},{10,14},{1... | collective-permute-start | bytes 1572872 | tf_op jit(solution)/shard_map/ppermute | solution.py:540
  107.3 49.8 %collective-permute-start.16 = (bf16[2,64,2048]{2,1,0:T(8,128)(2,1)S(1)}, bf16[2,64,2048]{2,1,0:T(8,128)(2,1)S(1)}, u32[]{:S(2)}, u32[]{:S(2)}) collective-permute-start(bf16[2,64,2048]{2,1,0:T(8,128)(2,1)S(1)} %get-tuple-element.133), channel_id=1, source_target_pairs={{0,6},{1,7},{2,4},{3,5},{4,2},{6,0},{7,1},{8,14},{9,15},{10,12},{1... | collective-permute-start | bytes 1572872 | tf_op jit(solution)/shard_map/ppermute | solution.py:540
  117.8 44.4 %collective-permute-start.19 = (bf16[2,48,2048]{2,1,0:T(8,128)(2,1)S(1)}, bf16[2,48,2048]{2,1,0:T(8,128)(2,1)S(1)}, u32[]{:S(2)}, u32[]{:S(2)}) collective-permute-start(bf16[2,48,2048]{2,1,0:T(8,128)(2,1)S(1)} %get-tuple-element.142), channel_id=1, source_target_pairs={{0,14},{1,15},{2,12},{4,10},{6,8},{7,9},{8,6},{10,4},{11,5},{12,2}... | collective-permute-start | bytes 1179656 | tf_op jit(solution)/shard_map/ppermute | solution.py:540
  119.2 43.1 %collective-permute-start.18 = (bf16[2,48,2048]{2,1,0:T(8,128)(2,1)S(1)}, bf16[2,48,2048]{2,1,0:T(8,128)(2,1)S(1)}, u32[]{:S(2)}, u32[]{:S(2)}) collective-permute-start(bf16[2,48,2048]{2,1,0:T(8,128)(2,1)S(1)} %get-tuple-element.141), channel_id=1, source_target_pairs={{0,12},{1,13},{2,14},{4,8},{6,10},{7,11},{8,4},{10,6},{11,7},{12,0... | collective-permute-start | bytes 1179656 | tf_op jit(solution)/shard_map/ppermute | solution.py:540
  157.7 10.7 %collective-permute-start.23 = (bf16[5,48,2048]{2,1,0:T(8,128)(2,1)S(1)}, bf16[5,48,2048]{2,1,0:T(8,128)(2,1)S(1)}, u32[]{:S(2)}, u32[]{:S(2)}) collective-permute-start(bf16[5,48,2048]{2,1,0:T(8,128)(2,1)S(1)} %get-tuple-element.144), channel_id=1, source_target_pairs={{0,1},{1,0},{2,3},{3,2},{4,5},{5,4},{6,7},{7,6},{8,9},{9,8},{10,11... | collective-permute-start | bytes 2949128 | tf_op jit(solution)/shard_map/ppermute | solution.py:540
  158.3 8.7 %collective-permute-start.21 = (bf16[2,32,2048]{2,1,0:T(8,128)(2,1)S(1)}, bf16[2,32,2048]{2,1,0:T(8,128)(2,1)S(1)}, u32[]{:S(2)}, u32[]{:S(2)}) collective-permute-start(bf16[2,32,2048]{2,1,0:T(8,128)(2,1)S(1)} %get-tuple-element.143), channel_id=1, source_target_pairs={{1,9},{3,11},{5,13},{7,15},{9,1},{11,3},{13,5},{15,7},{17,25},{19,... | collective-permute-start | bytes 786440 | tf_op jit(solution)/shard_map/ppermute | solution.py:540
  162.9 11.1 %collective-permute-start.20 = (bf16[4,48,2048]{2,1,0:T(8,128)(2,1)S(1)}, bf16[4,48,2048]{2,1,0:T(8,128)(2,1)S(1)}, u32[]{:S(2)}, u32[]{:S(2)}) collective-permute-start(bf16[4,48,2048]{2,1,0:T(8,128)(2,1)S(1)} %gather.2), channel_id=1, source_target_pairs={{0,1},{1,0},{2,3},{3,2},{4,5},{5,4},{6,7},{7,6},{8,9},{9,8},{10,11... | collective-permute-start | bytes 2359304 | tf_op jit(solution)/shard_map/ppermute | solution.py:540
  167.0 5.9 %collective-permute-start.22 = (bf16[32,2048]{1,0:T(8,128)(2,1)S(1)}, bf16[32,2048]{1,0:T(8,128)(2,1)S(1)}, u32[]{:S(2)}, u32[]{:S(2)}) collective-permute-start(bf16[32,2048]{1,0:T(8,128)(2,1)S(1)} %slice_bitcast_fusion), channel_id=1, source_target_pairs={{1,0},{3,2},{5,4},{7,6},{9,8},{11,10},{13,12},{15,14},{17,16},{19,... | collective-permute-start | bytes 393224 | tf_op jit(solution)/shard_map/ppermute | solution.py:540
  (12 other events, 78.5 us)

commit v3 on v1

--- a/solution.py
+++ b/solution.py
@@ -588,6 +588,7 @@
     far = cross(far, table, far_steps, True)
     for step in near_steps[1:]:
         near[step] = permute(near[step], block_pairs(table, step, True))
+        kv[step], near[step] = together(kv[step], near[step])
         kv[step] = permute(kv[step], block_pairs(table, step, True, (2,)))
     kinds = jnp.asarray(table[0])
 

time: 171 us -> 176 us (1.029)
  waiting for transfers between devices: 30.8 us -> 72 us
  starting transfers between devices: 84.6 us -> 45.7 us
  other arithmetic: 5.89 us -> 8.33 us
    ppermute x24, waiting for transfers between devices: 30.8 us -> 72 us  [permute(): return lax.ppermute(array, 'fsdp', pairs)]
    ppermute x24, starting transfers between devices: 84.6 us -> 45.7 us  [permute(): return lax.ppermute(array, 'fsdp', pairs)]
    add x1, other arithmetic: 4.34 us -> 6.78 us  [shards(): expert_moment_out = MOMENTUM * expert_momentum + factor * expert_grad]
  transfers between devices with their start and end apart: 24 -> 24, of which waited for: 7 -> 10; matrix products, arithmetic and copies ran while one was open for 4% -> 5% of each run, Pallas kernels for 9% -> 8%
where the time goes in v3:
time: 176 us; the launch traced here: 175 us
  waiting for transfers between devices  72 us (41%)
  starting transfers between devices  45.7 us (26%)
  Pallas kernels  32.6 us (19%)
  blocking collectives  14.6 us (8%)
  other arithmetic  8.33 us (5%)
    ppermute x24, waiting for transfers between devices, permute(): return lax.ppermute(array, 'fsdp', pairs)  72 us
    ppermute x24, starting transfers between devices, permute(): return lax.ppermute(array, 'fsdp', pairs)  45.7 us
    all_to_all x1, blocking collectives, shards(): squares = lax.all_to_all(partial, 'fsdp', 0, 0, tiled=True)  14.6 us
    pallas_call x3, Pallas kernels, finish(): pl.pallas_call(functools.partial(finish_kernel, (own, sibling is not None...  9.24 us
    pallas_call x1, Pallas kernels, orthogonal_update(): pl.pallas_call(functools.partial(transform_kernel, gain, kv_rows), in_spe...  8.92 us
    add x1, other arithmetic, shards(): expert_moment_out = MOMENTUM * expert_momentum + factor * expert_grad  6.78 us
    pallas_call x1, Pallas kernels, load(): pl.pallas_call(load_kernel, in_specs=[hbm] * 2, out_specs=[vmem] * 3, out...  3.86 us
  transfers between devices with their start and end apart: 24, of which 10 were waited for; matrix products, arithmetic and copies ran while one was open for 5% of the time, Pallas kernels for 8%

profile of v3, /device:TPU:1, one launch (start us, length us, event | category | flops | bytes accessed | tf_op | source)
XLA Modules:
  0.0 175.0 jit_solution(13088353836046784027)
XLA Ops:
  0.7 3.9 %load.1 = (f32[8,2048]{1,0:T(8,128)S(1)}, f32[12,48,2048]{2,1,0:T(8,128)S(1)}, f32[12,48,2048]{2,1,0:T(8,128)S(1)}) custom-call(f32[12,48,2048]{2,1,0:T(8,128)} %bitcast.20, f32[12,48,2048]{2,1,0:T(8,128)} %bitcast.23), custom_call_target="tpu_custom_call" | custom-call | tf_op jit(solution)/shard_map/load/pallas_call | solution.py:99
  5.7 3.8 %collective-permute-start.1 = (bf16[2,32,2048]{2,1,0:T(8,128)(2,1)S(1)}, bf16[2,32,2048]{2,1,0:T(8,128)(2,1)S(1)}, u32[]{:S(2)}, u32[]{:S(2)}) collective-permute-start(bf16[2,32,2048]{2,1,0:T(8,128)(2,1)S(1)} %get-tuple-element.92), channel_id=1, source_target_pairs={{0,8},{1,9},{2,10},{3,11},{4,12},{5,13},{6,14},{7,15},{8,0},{9,1},... | collective-permute-start | bytes 786440 | tf_op jit(solution)/shard_map/ppermute | solution.py:538
  9.5 14.6 %all_to_all.5.squares = f32[16,8,128]{2,1,0:T(8,128)S(1)} all-to-all(f32[16,8,128]{2,1,0:T(8,128)S(1)} %get-tuple-element.90), channel_id=1, replica_groups=mesh['groups'=2,'fsdp'=16] {'fsdp'}, dimensions={0} | all-to-all | bytes 131072 | tf_op jit(solution)/shard_map/all_to_all | solution.py:579
  26.7 4.2 %collective-permute-start.10 = (bf16[2,48,2048]{2,1,0:T(8,128)(2,1)S(1)}, bf16[2,48,2048]{2,1,0:T(8,128)(2,1)S(1)}, u32[]{:S(2)}, u32[]{:S(2)}) collective-permute-start(bf16[2,48,2048]{2,1,0:T(8,128)(2,1)S(1)} %get-tuple-element.122), channel_id=1, source_target_pairs={{10,0},{11,1},{8,2},{14,4},{12,6},{13,7},{2,8},{0,10},{1,11},{6,12... | collective-permute-start | bytes 1179656 | tf_op jit(solution)/shard_map/ppermute | solution.py:538
  32.8 1.6 form.1
  34.4 4.0 %collective-permute-start.5 = (bf16[2,48,2048]{2,1,0:T(8,128)(2,1)S(1)}, bf16[2,48,2048]{2,1,0:T(8,128)(2,1)S(1)}, u32[]{:S(2)}, u32[]{:S(2)}) collective-permute-start(bf16[2,48,2048]{2,1,0:T(8,128)(2,1)S(1)} %get-tuple-element.110), channel_id=1, source_target_pairs={{6,0},{7,1},{4,2},{2,4},{0,6},{1,7},{14,8},{12,10},{13,11},{10,12}... | collective-permute-start | bytes 1179656 | tf_op jit(solution)/shard_map/ppermute | solution.py:538
  41.1 6.8 %multiply_add_fusion = f32[4,3,48,2048]{3,2,1,0:T(8,128)} fusion(f32[4,3,48,2048]{3,2,1,0:T(8,128)S(1)} %bitcast.22, f32[4,3,48,2048]{3,2,1,0:T(8,128)} %param.21, f32[]{:T(128)} %bitcast.5), kind=kLoop, calls=%fused_computation | loop fusion | flops 3538944 | bytes 14155780 | tf_op jit(solution)/shard_map/add | solution.py:596
  47.8 4.7 %collective-permute-done.10.refs_5_ = bf16[2,48,2048]{2,1,0:T(8,128)(2,1)S(1)} collective-permute-done((bf16[2,48,2048]{2,1,0:T(8,128)(2,1)S(1)}, bf16[2,48,2048]{2,1,0:T(8,128)(2,1)S(1)}, u32[]{:S(2)}, u32[]{:S(2)}) %collective-permute-start.10) | collective-permute-done | bytes 393248 | tf_op jit(solution)/shard_map/ppermute | solution.py:538
  54.3 4.6 %collective-permute-start.11 = (bf16[2,48,2048]{2,1,0:T(8,128)(2,1)S(1)}, bf16[2,48,2048]{2,1,0:T(8,128)(2,1)S(1)}, u32[]{:S(2)}, u32[]{:S(2)}) collective-permute-start(bf16[2,48,2048]{2,1,0:T(8,128)(2,1)S(1)} %get-tuple-element.124), channel_id=1, source_target_pairs={{12,0},{13,1},{14,2},{8,4},{10,6},{11,7},{4,8},{6,10},{7,11},{0,12... | collective-permute-start | bytes 1179656 | tf_op jit(solution)/shard_map/ppermute | solution.py:538
  59.0 12.1 %collective-permute-done.4.refs_2_ = bf16[2,48,2048]{2,1,0:T(8,128)(2,1)S(1)} collective-permute-done((bf16[2,48,2048]{2,1,0:T(8,128)(2,1)S(1)}, bf16[2,48,2048]{2,1,0:T(8,128)(2,1)S(1)}, u32[]{:S(2)}, u32[]{:S(2)}) %collective-permute-start.4) | collective-permute-done | bytes 393248 | tf_op jit(solution)/shard_map/ppermute | solution.py:538
  73.0 2.3 %collective-permute-start.6 = (bf16[2,64,2048]{2,1,0:T(8,128)(2,1)S(1)}, bf16[2,64,2048]{2,1,0:T(8,128)(2,1)S(1)}, u32[]{:S(2)}, u32[]{:S(2)}) collective-permute-start(bf16[2,64,2048]{2,1,0:T(8,128)(2,1)S(1)} %get-tuple-element.115), channel_id=1, source_target_pairs={{1,3},{11,9},{17,19},{27,25}} | collective-permute-start | bytes 1572872 | tf_op jit(solution)/shard_map/ppermute | solution.py:538
  75.3 1.5 multiply_add_fusion.1
  76.8 1.5 near.1
  78.4 7.4 %collective-permute-done.6.refs_1_ = bf16[2,64,2048]{2,1,0:T(8,128)(2,1)S(1)} collective-permute-done((bf16[2,64,2048]{2,1,0:T(8,128)(2,1)S(1)}, bf16[2,64,2048]{2,1,0:T(8,128)(2,1)S(1)}, u32[]{:S(2)}, u32[]{:S(2)}) %collective-permute-start.6) | collective-permute-done | bytes 524320 | tf_op jit(solution)/shard_map/ppermute | solution.py:538
  85.8 8.9 %transform.1 = (bf16[768,2048]{1,0:T(8,128)(2,1)S(1)}, bf16[768,768]{1,0:T(8,128)(2,1)S(1)}, f32[768,128]{1,0:T(8,128)S(1)}, bf16[2,48,2048]{2,1,0:T(8,128)(2,1)S(1)}, bf16[2,48,2048]{2,1,0:T(8,128)(2,1)S(1)}) custom-call(s32[1]{0:T(128)} %bitcast.me, s32[16]{0:T(128)S(1)} %copy-done.5, bf16[384,2048]{1,0:T(8,128)(2,1)S(1)} %get-tuple-element.112.near, ...), custom_call_target="tpu_custom_call" | custom-call | tf_op jit(solution)/shard_map/transform/pallas_call | solution.py:365
  94.8 1.9 %collective-permute-start.17 = (bf16[2,48,2048]{2,1,0:T(8,128)(2,1)S(1)}, bf16[2,48,2048]{2,1,0:T(8,128)(2,1)S(1)}, u32[]{:S(2)}, u32[]{:S(2)}) collective-permute-start(bf16[2,48,2048]{2,1,0:T(8,128)(2,1)S(1)} %get-tuple-element.141), channel_id=1, source_target_pairs={{0,10},{1,11},{2,8},{4,14},{6,12},{7,13},{8,2},{10,0},{11,1},{12,6... | collective-permute-start | bytes 1179656 | tf_op jit(solution)/shard_map/ppermute | solution.py:538
  96.7 1.3 collective-permute-start.13
  98.0 2.9 %apply.1 = (bf16[2,64,2048]{2,1,0:T(8,128)(2,1)S(1)}, bf16[2,64,2048]{2,1,0:T(8,128)(2,1)S(1)}, bf16[2,64,2048]{2,1,0:T(8,128)(2,1)S(1)}, bf16[2,64,2048]{2,1,0:...) custom-call(s32[1]{0:T(128)} %bitcast.me, s32[16]{0:T(128)S(1)} %copy-done.5, ...), custom_call_target="tpu_custom_call" | custom-call | tf_op jit(solution)/shard_map/apply/pallas_call | solution.py:380
  101.0 1.9 %collective-permute-start.14 = (bf16[2,64,2048]{2,1,0:T(8,128)(2,1)S(1)}, bf16[2,64,2048]{2,1,0:T(8,128)(2,1)S(1)}, u32[]{:S(2)}, u32[]{:S(2)}) collective-permute-start(bf16[2,64,2048]{2,1,0:T(8,128)(2,1)S(1)} %get-tuple-element.133), channel_id=1, source_target_pairs={{0,2},{1,3},{2,0},{3,1},{4,6},{6,4},{7,5},{8,10},{9,11},{10,8},{11... | collective-permute-start | bytes 1572872 | tf_op jit(solution)/shard_map/ppermute | solution.py:538
  102.9 1.3 collective-permute-start.15
  104.2 5.1 %collective-permute-start.16 = (bf16[2,64,2048]{2,1,0:T(8,128)(2,1)S(1)}, bf16[2,64,2048]{2,1,0:T(8,128)(2,1)S(1)}, u32[]{:S(2)}, u32[]{:S(2)}) collective-permute-start(bf16[2,64,2048]{2,1,0:T(8,128)(2,1)S(1)} %get-tuple-element.135), channel_id=1, source_target_pairs={{0,6},{1,7},{2,4},{3,5},{4,2},{6,0},{7,1},{8,14},{9,15},{10,12},{1... | collective-permute-start | bytes 1572872 | tf_op jit(solution)/shard_map/ppermute | solution.py:538
  109.4 7.4 %collective-permute-done.17.refs_1_ = bf16[2,48,2048]{2,1,0:T(8,128)(2,1)S(1)} collective-permute-done((bf16[2,48,2048]{2,1,0:T(8,128)(2,1)S(1)}, bf16[2,48,2048]{2,1,0:T(8,128)(2,1)S(1)}, u32[]{:S(2)}, u32[]{:S(2)}) %collective-permute-start.17) | collective-permute-done | bytes 393248 | tf_op jit(solution)/shard_map/ppermute | solution.py:538
  116.7 1.3 collective-permute-start.19
  118.1 1.9 %collective-permute-start.18 = (bf16[2,48,2048]{2,1,0:T(8,128)(2,1)S(1)}, bf16[2,48,2048]{2,1,0:T(8,128)(2,1)S(1)}, u32[]{:S(2)}, u32[]{:S(2)}) collective-permute-start(bf16[2,48,2048]{2,1,0:T(8,128)(2,1)S(1)} %get-tuple-element.143), channel_id=1, source_target_pairs={{0,12},{1,13},{2,14},{4,8},{6,10},{7,11},{8,4},{10,6},{11,7},{12,0... | collective-permute-start | bytes 1179656 | tf_op jit(solution)/shard_map/ppermute | solution.py:538
  120.0 1.9 %collective-permute-done.14.refs_1_ = bf16[2,64,2048]{2,1,0:T(8,128)(2,1)S(1)} collective-permute-done((bf16[2,64,2048]{2,1,0:T(8,128)(2,1)S(1)}, bf16[2,64,2048]{2,1,0:T(8,128)(2,1)S(1)}, u32[]{:S(2)}, u32[]{:S(2)}) %collective-permute-start.14) | collective-permute-done | bytes 524320 | tf_op jit(solution)/shard_map/ppermute | solution.py:538
  123.0 33.0 %collective-permute-done.16.refs_3_ = bf16[2,64,2048]{2,1,0:T(8,128)(2,1)S(1)} collective-permute-done((bf16[2,64,2048]{2,1,0:T(8,128)(2,1)S(1)}, bf16[2,64,2048]{2,1,0:T(8,128)(2,1)S(1)}, u32[]{:S(2)}, u32[]{:S(2)}) %collective-permute-start.16) | collective-permute-done | bytes 524320 | tf_op jit(solution)/shard_map/ppermute | solution.py:538
  157.1 1.9 %collective-permute-start.21 = (bf16[2,32,2048]{2,1,0:T(8,128)(2,1)S(1)}, bf16[2,32,2048]{2,1,0:T(8,128)(2,1)S(1)}, u32[]{:S(2)}, u32[]{:S(2)}) collective-permute-start(bf16[2,32,2048]{2,1,0:T(8,128)(2,1)S(1)} %get-tuple-element.145), channel_id=1, source_target_pairs={{1,9},{3,11},{5,13},{7,15},{9,1},{11,3},{13,5},{15,7},{17,25},{19,... | collective-permute-start | bytes 786440 | tf_op jit(solution)/shard_map/ppermute | solution.py:538
  159.1 2.0 %finish.3 = (f32[12,48,2048]{2,1,0:T(8,128)}, bf16[12,48,2048]{2,1,0:T(8,128)(2,1)}, bf16[12,48,2048]{2,1,0:T(8,128)(2,1)}) custom-call(s32[1]{0:T(128)} %bitcast.me, s32[64]{0:T(128)S(1)} %copy-done.3, s32[64]{0:T(128)S(1)} %copy-done.4, bf16[2,64,2048]{2,1,0:T(8,128)(2,1)S(1)} %get-tuple-element.132.refs_0_, ...), custom_call_target="tpu_custom_call" | custom-call | tf_op jit(solution)/shard_map/finish/pallas_call | solution.py:520
  161.8 3.3 %collective-permute-done.21.across = bf16[2,32,2048]{2,1,0:T(8,128)(2,1)S(1)} collective-permute-done((bf16[2,32,2048]{2,1,0:T(8,128)(2,1)S(1)}, bf16[2,32,2048]{2,1,0:T(8,128)(2,1)S(1)}, u32[]{:S(2)}, u32[]{:S(2)}) %collective-permute-start.21) | collective-permute-done | bytes 262176 | tf_op jit(solution)/shard_map/ppermute | solution.py:538
  165.2 1.4 collective-permute-start.22
  166.7 4.5 %finish.4 = (f32[12,48,2048]{2,1,0:T(8,128)}, bf16[12,48,2048]{2,1,0:T(8,128)(2,1)}, bf16[12,48,2048]{2,1,0:T(8,128)(2,1)}) custom-call(s32[1]{0:T(128)} %bitcast.me, s32[128]{0:T(128)S(1)} %copy-done.9, s32[128]{0:T(128)S(1)} %copy-done.10, ...), custom_call_target="tpu_custom_call", output_to_operand_aliasing={{0}: (9, {}), {1}: (10, {}), {2}: (11, {})} | custom-call | tf_op jit(solution)/shard_map/finish/pallas_call | solution.py:520
  172.2 2.8 %finish.5 = (f32[12,48,2048]{2,1,0:T(8,128)}, bf16[12,48,2048]{2,1,0:T(8,128)(2,1)}, bf16[12,48,2048]{2,1,0:T(8,128)(2,1)}) custom-call(s32[1]{0:T(128)} %bitcast.me, s32[64]{0:T(128)S(1)} %copy-done.7, s32[64]{0:T(128)S(1)} %copy-done.8, ...), custom_call_target="tpu_custom_call", output_to_operand_aliasing={{0}: (5, {}), {1}: (6, {}), {2}: (7, {})} | custom-call | tf_op jit(solution)/shard_map/finish/pallas_call | solution.py:520
  (71 shorter events, 16.0 us)
Async XLA Ops:
  4.6 19.5 %copy-start.6 = (s32[64]{0:T(128)S(1)}, s32[64]{0:T(128)}, u32[]{:S(2)}) copy-start(s32[64]{0:T(128)} %constant.28.clone.kinds) | copy-start | bytes 772
  4.6 19.5 %copy-start.11 = (s32[64]{0:T(128)S(1)}, s32[64]{0:T(128)}, u32[]{:S(2)}) copy-start(s32[64]{0:T(128)} %constant.29.clone.index) | copy-start | bytes 772
  5.6 18.5 %collective-permute-start = (bf16[2,8,48,2048]{3,2,1,0:T(8,128)(2,1)S(1)}, bf16[2,8,48,2048]{3,2,1,0:T(8,128)(2,1)S(1)}, u32[]{:S(2)}, u32[]{:S(2)}) collective-permute-start(bf16[2,8,48,2048]{3,2,1,0:T(8,128)(2,1)S(1)} %get-tuple-element.91), channel_id=1, source_target_pairs={{0,1},{1,0},{2,3},{3,2},{4,5},{5,4},{6,7},{7,6},{8,9},{9,8},{10,11... | collective-permute-start | bytes 9437192 | tf_op jit(solution)/shard_map/ppermute | solution.py:538
  5.7 18.4 %collective-permute-start.1 = (bf16[2,32,2048]{2,1,0:T(8,128)(2,1)S(1)}, bf16[2,32,2048]{2,1,0:T(8,128)(2,1)S(1)}, u32[]{:S(2)}, u32[]{:S(2)}) collective-permute-start(bf16[2,32,2048]{2,1,0:T(8,128)(2,1)S(1)} %get-tuple-element.92), channel_id=1, source_target_pairs={{0,8},{1,9},{2,10},{3,11},{4,12},{5,13},{6,14},{7,15},{8,0},{9,1},... | collective-permute-start | bytes 786440 | tf_op jit(solution)/shard_map/ppermute | solution.py:538
  24.1 8.7 %copy-start.3 = (s32[64]{0:T(128)S(1)}, s32[64]{0:T(128)}, u32[]{:S(2)}) copy-start(s32[64]{0:T(128)} %constant.30.clone.kinds) | copy-start | bytes 772
  24.1 8.7 %copy-start.4 = (s32[64]{0:T(128)S(1)}, s32[64]{0:T(128)}, u32[]{:S(2)}) copy-start(s32[64]{0:T(128)} %constant.31.clone.index.held) | copy-start | bytes 772
  25.4 7.4 %collective-permute-start.2 = (bf16[2,2,32,2048]{3,2,1,0:T(8,128)(2,1)S(1)}, bf16[2,2,32,2048]{3,2,1,0:T(8,128)(2,1)S(1)}, u32[]{:S(2)}, u32[]{:S(2)}) collective-permute-start(bf16[2,2,32,2048]{3,2,1,0:T(8,128)(2,1)S(1)} %pad_maximum_fusion), channel_id=1, source_target_pairs={{0,1},{2,3},{4,5},{6,7},{8,9},{10,11},{12,13},{14,15},{16,17},{18,... | collective-permute-start | bytes 1572872 | tf_op jit(solution)/shard_map/ppermute | solution.py:538
  26.7 25.8 %collective-permute-start.10 = (bf16[2,48,2048]{2,1,0:T(8,128)(2,1)S(1)}, bf16[2,48,2048]{2,1,0:T(8,128)(2,1)S(1)}, u32[]{:S(2)}, u32[]{:S(2)}) collective-permute-start(bf16[2,48,2048]{2,1,0:T(8,128)(2,1)S(1)} %get-tuple-element.122), channel_id=1, source_target_pairs={{10,0},{11,1},{8,2},{14,4},{12,6},{13,7},{2,8},{0,10},{1,11},{6,12... | collective-permute-start | bytes 1179656 | tf_op jit(solution)/shard_map/ppermute | solution.py:538
  30.9 23.4 %collective-permute-start.9 = (bf16[2,48,2048]{2,1,0:T(8,128)(2,1)S(1)}, bf16[2,48,2048]{2,1,0:T(8,128)(2,1)S(1)}, u32[]{:S(2)}, u32[]{:S(2)}) collective-permute-start(bf16[2,48,2048]{2,1,0:T(8,128)(2,1)S(1)} %get-tuple-element.119), channel_id=1, source_target_pairs={{8,0},{9,1},{10,2},{12,4},{14,6},{15,7},{0,8},{2,10},{3,11},{4,12}... | collective-permute-start | bytes 1179656 | tf_op jit(solution)/shard_map/ppermute | solution.py:538
  32.2 8.8 %slice-start.2 = ((s8[4718592]{0:T(1024)(128)(4,1)}), s8[4194304]{0:T(1024)(128)(4,1)S(1)}, s32[]{:S(2)}) async-start(s8[4718592]{0:T(1024)(128)(4,1)} %bitcast.21), calls=%async_computation.3 | async-start | bytes 8388608
  34.4 24.6 %collective-permute-start.5 = (bf16[2,48,2048]{2,1,0:T(8,128)(2,1)S(1)}, bf16[2,48,2048]{2,1,0:T(8,128)(2,1)S(1)}, u32[]{:S(2)}, u32[]{:S(2)}) collective-permute-start(bf16[2,48,2048]{2,1,0:T(8,128)(2,1)S(1)} %get-tuple-element.110), channel_id=1, source_target_pairs={{6,0},{7,1},{4,2},{2,4},{0,6},{1,7},{14,8},{12,10},{13,11},{10,12}... | collective-permute-start | bytes 1179656 | tf_op jit(solution)/shard_map/ppermute | solution.py:538
  38.4 32.6 %collective-permute-start.4 = (bf16[2,48,2048]{2,1,0:T(8,128)(2,1)S(1)}, bf16[2,48,2048]{2,1,0:T(8,128)(2,1)S(1)}, u32[]{:S(2)}, u32[]{:S(2)}) collective-permute-start(bf16[2,48,2048]{2,1,0:T(8,128)(2,1)S(1)} %get-tuple-element.107), channel_id=1, source_target_pairs={{4,0},{5,1},{6,2},{0,4},{2,6},{3,7},{12,8},{14,10},{15,11},{8,12},... | collective-permute-start | bytes 1179656 | tf_op jit(solution)/shard_map/ppermute | solution.py:538
  39.7 31.9 %collective-permute-start.3 = (bf16[2,48,2048]{2,1,0:T(8,128)(2,1)S(1)}, bf16[2,48,2048]{2,1,0:T(8,128)(2,1)S(1)}, u32[]{:S(2)}, u32[]{:S(2)}) collective-permute-start(bf16[2,48,2048]{2,1,0:T(8,128)(2,1)S(1)} %get-tuple-element.104), channel_id=1, source_target_pairs={{2,0},{3,1},{0,2},{6,4},{4,6},{5,7},{10,8},{8,10},{9,11},{14,12},{... | collective-permute-start | bytes 1179656 | tf_op jit(solution)/shard_map/ppermute | solution.py:538
  41.0 35.8 %copy-start.5 = (s32[16]{0:T(128)S(1)}, s32[16]{0:T(128)}, u32[]{:S(2)}) copy-start(s32[16]{0:T(128)} %constant.32.clone.kinds) | copy-start | bytes 196
  52.5 25.9 %collective-permute-start.12 = (bf16[2,48,2048]{2,1,0:T(8,128)(2,1)S(1)}, bf16[2,48,2048]{2,1,0:T(8,128)(2,1)S(1)}, u32[]{:S(2)}, u32[]{:S(2)}) collective-permute-start(bf16[2,48,2048]{2,1,0:T(8,128)(2,1)S(1)} %get-tuple-element.125), channel_id=1, source_target_pairs={{14,0},{15,1},{12,2},{10,4},{8,6},{9,7},{6,8},{4,10},{5,11},{2,12}... | collective-permute-start | bytes 1179656 | tf_op jit(solution)/shard_map/ppermute | solution.py:538
  54.3 24.1 %collective-permute-start.11 = (bf16[2,48,2048]{2,1,0:T(8,128)(2,1)S(1)}, bf16[2,48,2048]{2,1,0:T(8,128)(2,1)S(1)}, u32[]{:S(2)}, u32[]{:S(2)}) collective-permute-start(bf16[2,48,2048]{2,1,0:T(8,128)(2,1)S(1)} %get-tuple-element.124), channel_id=1, source_target_pairs={{12,0},{13,1},{14,2},{8,4},{10,6},{11,7},{4,8},{6,10},{7,11},{0,12... | collective-permute-start | bytes 1179656 | tf_op jit(solution)/shard_map/ppermute | solution.py:538
  71.7 6.7 %collective-permute-start.8 = (bf16[2,64,2048]{2,1,0:T(8,128)(2,1)S(1)}, bf16[2,64,2048]{2,1,0:T(8,128)(2,1)S(1)}, u32[]{:S(2)}, u32[]{:S(2)}) collective-permute-start(bf16[2,64,2048]{2,1,0:T(8,128)(2,1)S(1)} %get-tuple-element.117), channel_id=1, source_target_pairs={{5,3},{15,9},{21,19},{31,25}} | collective-permute-start | bytes 1572872 | tf_op jit(solution)/shard_map/ppermute | solution.py:538
  72.3 6.1 %collective-permute-start.7 = (bf16[2,64,2048]{2,1,0:T(8,128)(2,1)S(1)}, bf16[2,64,2048]{2,1,0:T(8,128)(2,1)S(1)}, u32[]{:S(2)}, u32[]{:S(2)}) collective-permute-start(bf16[2,64,2048]{2,1,0:T(8,128)(2,1)S(1)} %get-tuple-element.116), channel_id=1, source_target_pairs={{7,3},{13,9},{23,19},{29,25}} | collective-permute-start | bytes 1572872 | tf_op jit(solution)/shard_map/ppermute | solution.py:538
  73.0 12.8 %collective-permute-start.6 = (bf16[2,64,2048]{2,1,0:T(8,128)(2,1)S(1)}, bf16[2,64,2048]{2,1,0:T(8,128)(2,1)S(1)}, u32[]{:S(2)}, u32[]{:S(2)}) collective-permute-start(bf16[2,64,2048]{2,1,0:T(8,128)(2,1)S(1)} %get-tuple-element.115), channel_id=1, source_target_pairs={{1,3},{11,9},{17,19},{27,25}} | collective-permute-start | bytes 1572872 | tf_op jit(solution)/shard_map/ppermute | solution.py:538
  76.8 82.2 %slice-start = ((s8[4718592]{0:T(1024)(128)(4,1)}), s8[4194304]{0:T(1024)(128)(4,1)S(1)}, s32[]{:S(2)}) async-start(s8[4718592]{0:T(1024)(128)(4,1)} %bitcast.12), calls=%async_computation.1 | async-start | bytes 8388608
  85.8 73.2 %slice-start.1 = ((s8[4718592]{0:T(1024)(128)(4,1)}), s8[524288]{0:T(1024)(128)(4,1)S(1)}, s32[]{:S(2)}) async-start(s8[4718592]{0:T(1024)(128)(4,1)} %bitcast.12), calls=%async_computation.2 | async-start | bytes 1048576
  94.8 22.0 %collective-permute-start.17 = (bf16[2,48,2048]{2,1,0:T(8,128)(2,1)S(1)}, bf16[2,48,2048]{2,1,0:T(8,128)(2,1)S(1)}, u32[]{:S(2)}, u32[]{:S(2)}) collective-permute-start(bf16[2,48,2048]{2,1,0:T(8,128)(2,1)S(1)} %get-tuple-element.141), channel_id=1, source_target_pairs={{0,10},{1,11},{2,8},{4,14},{6,12},{7,13},{8,2},{10,0},{11,1},{12,6... | collective-permute-start | bytes 1179656 | tf_op jit(solution)/shard_map/ppermute | solution.py:538
  96.7 21.4 %collective-permute-start.13 = (bf16[2,48,2048]{2,1,0:T(8,128)(2,1)S(1)}, bf16[2,48,2048]{2,1,0:T(8,128)(2,1)S(1)}, u32[]{:S(2)}, u32[]{:S(2)}) collective-permute-start(bf16[2,48,2048]{2,1,0:T(8,128)(2,1)S(1)} %get-tuple-element.130), channel_id=1, source_target_pairs={{0,8},{1,9},{2,10},{4,12},{6,14},{7,15},{8,0},{10,2},{11,3},{12,4}... | collective-permute-start | bytes 1179656 | tf_op jit(solution)/shard_map/ppermute | solution.py:538
  101.0 21.0 %collective-permute-start.14 = (bf16[2,64,2048]{2,1,0:T(8,128)(2,1)S(1)}, bf16[2,64,2048]{2,1,0:T(8,128)(2,1)S(1)}, u32[]{:S(2)}, u32[]{:S(2)}) collective-permute-start(bf16[2,64,2048]{2,1,0:T(8,128)(2,1)S(1)} %get-tuple-element.133), channel_id=1, source_target_pairs={{0,2},{1,3},{2,0},{3,1},{4,6},{6,4},{7,5},{8,10},{9,11},{10,8},{11... | collective-permute-start | bytes 1572872 | tf_op jit(solution)/shard_map/ppermute | solution.py:538
  102.9 20.1 %collective-permute-start.15 = (bf16[2,64,2048]{2,1,0:T(8,128)(2,1)S(1)}, bf16[2,64,2048]{2,1,0:T(8,128)(2,1)S(1)}, u32[]{:S(2)}, u32[]{:S(2)}) collective-permute-start(bf16[2,64,2048]{2,1,0:T(8,128)(2,1)S(1)} %get-tuple-element.134), channel_id=1, source_target_pairs={{0,4},{1,5},{2,6},{3,7},{4,0},{6,2},{7,3},{8,12},{9,13},{10,14},{1... | collective-permute-start | bytes 1572872 | tf_op jit(solution)/shard_map/ppermute | solution.py:538
  104.2 51.8 %collective-permute-start.16 = (bf16[2,64,2048]{2,1,0:T(8,128)(2,1)S(1)}, bf16[2,64,2048]{2,1,0:T(8,128)(2,1)S(1)}, u32[]{:S(2)}, u32[]{:S(2)}) collective-permute-start(bf16[2,64,2048]{2,1,0:T(8,128)(2,1)S(1)} %get-tuple-element.135), channel_id=1, source_target_pairs={{0,6},{1,7},{2,4},{3,5},{4,2},{6,0},{7,1},{8,14},{9,15},{10,12},{1... | collective-permute-start | bytes 1572872 | tf_op jit(solution)/shard_map/ppermute | solution.py:538
  116.7 44.4 %collective-permute-start.19 = (bf16[2,48,2048]{2,1,0:T(8,128)(2,1)S(1)}, bf16[2,48,2048]{2,1,0:T(8,128)(2,1)S(1)}, u32[]{:S(2)}, u32[]{:S(2)}) collective-permute-start(bf16[2,48,2048]{2,1,0:T(8,128)(2,1)S(1)} %get-tuple-element.144), channel_id=1, source_target_pairs={{0,14},{1,15},{2,12},{4,10},{6,8},{7,9},{8,6},{10,4},{11,5},{12,2}... | collective-permute-start | bytes 1179656 | tf_op jit(solution)/shard_map/ppermute | solution.py:538
  118.1 43.1 %collective-permute-start.18 = (bf16[2,48,2048]{2,1,0:T(8,128)(2,1)S(1)}, bf16[2,48,2048]{2,1,0:T(8,128)(2,1)S(1)}, u32[]{:S(2)}, u32[]{:S(2)}) collective-permute-start(bf16[2,48,2048]{2,1,0:T(8,128)(2,1)S(1)} %get-tuple-element.143), channel_id=1, source_target_pairs={{0,12},{1,13},{2,14},{4,8},{6,10},{7,11},{8,4},{10,6},{11,7},{12,0... | collective-permute-start | bytes 1179656 | tf_op jit(solution)/shard_map/ppermute | solution.py:538
  156.6 10.0 %collective-permute-start.23 = (bf16[5,48,2048]{2,1,0:T(8,128)(2,1)S(1)}, bf16[5,48,2048]{2,1,0:T(8,128)(2,1)S(1)}, u32[]{:S(2)}, u32[]{:S(2)}) collective-permute-start(bf16[5,48,2048]{2,1,0:T(8,128)(2,1)S(1)} %get-tuple-element.146), channel_id=1, source_target_pairs={{0,1},{1,0},{2,3},{3,2},{4,5},{5,4},{6,7},{7,6},{8,9},{9,8},{10,11... | collective-permute-start | bytes 2949128 | tf_op jit(solution)/shard_map/ppermute | solution.py:538
  157.1 8.0 %collective-permute-start.21 = (bf16[2,32,2048]{2,1,0:T(8,128)(2,1)S(1)}, bf16[2,32,2048]{2,1,0:T(8,128)(2,1)S(1)}, u32[]{:S(2)}, u32[]{:S(2)}) collective-permute-start(bf16[2,32,2048]{2,1,0:T(8,128)(2,1)S(1)} %get-tuple-element.145), channel_id=1, source_target_pairs={{1,9},{3,11},{5,13},{7,15},{9,1},{11,3},{13,5},{15,7},{17,25},{19,... | collective-permute-start | bytes 786440 | tf_op jit(solution)/shard_map/ppermute | solution.py:538
  161.7 10.5 %collective-permute-start.20 = (bf16[4,48,2048]{2,1,0:T(8,128)(2,1)S(1)}, bf16[4,48,2048]{2,1,0:T(8,128)(2,1)S(1)}, u32[]{:S(2)}, u32[]{:S(2)}) collective-permute-start(bf16[4,48,2048]{2,1,0:T(8,128)(2,1)S(1)} %gather.2), channel_id=1, source_target_pairs={{0,1},{1,0},{2,3},{3,2},{4,5},{5,4},{6,7},{7,6},{8,9},{9,8},{10,11... | collective-permute-start | bytes 2359304 | tf_op jit(solution)/shard_map/ppermute | solution.py:538
  165.2 5.9 %collective-permute-start.22 = (bf16[32,2048]{1,0:T(8,128)(2,1)S(1)}, bf16[32,2048]{1,0:T(8,128)(2,1)S(1)}, u32[]{:S(2)}, u32[]{:S(2)}) collective-permute-start(bf16[32,2048]{1,0:T(8,128)(2,1)S(1)} %slice_bitcast_fusion), channel_id=1, source_target_pairs={{1,0},{3,2},{5,4},{7,6},{9,8},{11,10},{13,12},{15,14},{17,16},{19,... | collective-permute-start | bytes 393224 | tf_op jit(solution)/shard_map/ppermute | solution.py:538
  (9 other events, 55.2 us)
